TPU v7x, 32 devices: a whole 2x2x4 slice. The times are simulated.
32 devices in a mesh: req: 8 (over z, y), mdl: 4 (over x, core).
Axes of the slice: x: 2, y: 2, z: 4, core: 2. Of those that a mesh axis runs over, the one named last changes fastest.
Arguments:
- stream: bfloat16 [6144, 1792], P('req'), may hold values from -6 to 6
- attention_projection_weight: bfloat16 [3, 1792, 1792], P(None, 'mdl'), may hold values from -0.125 to 0.125
- head_output_weight: bfloat16 [1792, 1792], P('mdl'), may hold values from -0.125 to 0.125
- adapter_down_maps: bfloat16 [64, 1792, 16], P('mdl'), may hold values from -0.125 to 0.125
- adapter_up_maps: bfloat16 [2, 1792, 1024], P(None, 'mdl'), may hold values from -1.5 to 1.5
- tenant_adapter_scale: float32 [4], replicated, may hold values from 0.5 to 2
- feedforward_norm_gain: bfloat16 [1792], replicated, may hold values from 0.099609375 to 1.8984375
- feedforward_weight: bfloat16 [3, 1792, 4864], P(None, 'req', 'mdl'), may hold values from -0.125 to 0.125
- prefix_cache_store: bfloat16 [256, 2, 1792, 128], P('req', None, 'mdl'), may hold values from -140 to 140
- token_adapter_index: int32 [6144], P('req'), may hold values from 0 to 63
- request_token_lengths: int32 [8, 24], P('req'), may hold values from 1 to 192, 768 in all within a row
- request_tenant_index: int32 [192], P('req'), may hold values from 0 to 3
- last_page_holder: int32 [192, 1], replicated, may hold values from 0 to 7; in each aligned block of 24 rows (0 to 23, 24 to 47, ...) at most 4 rows name the same one
- holder_page_slot: int32 [192], replicated, may hold values from 0 to 31
- page_filled_rows: int32 [192], replicated, may hold values from 64 to 128
Outputs:
- layer_out: bfloat16 [6144, 1792], P(('req', 'mdl'))
Inputs may be any that keep to these rules, and one draw needn't show every extreme that they name: `last_page_holder`: within the rows of one index of req (aligned blocks of 24 rows) no holder is named more than 4 times, and one holder exactly 4 times in some blocks. `request_token_lengths`: each row sums to 768; its longest request has exactly 192 tokens.
All inputs are finite; a program needn't handle non-finite values.
Results may differ from a plain program's by a relative error of at most 0.025.
Values may be sent and summed in bfloat16 or wider, within the bound.
No kernel may reach another device: no remote copies, remote signals or barrier semaphores. Data moves between devices by JAX's collectives and lax.ppermute only.
A program may use at most 128 MiB of HBM per device.

v0:
```python
import functools
import math

import jax
import jax.numpy as jnp
from jax import lax
from jax.experimental import pallas as pl
from jax.experimental.pallas import tpu as pltpu
from jax.sharding import PartitionSpec as P

HEAD_SIZE = 112
WINDOW = 64
BLOCK = 192
HALO = 64
LANES = 256
VMEM_LIMIT = 48 * 1024 * 1024
NT = (((1,), (1,)), ((), ()))
SMALL = pl.CostEstimate(flops=0, bytes_accessed=0, transcendentals=0)


def pack_kernel(cap, table_ref, offset_ref, *refs):
    page_refs, out_ref = refs[:cap], refs[cap]
    dest = pl.program_id(0)
    lane = lax.broadcasted_iota(jnp.int32, out_ref.shape[3:], 1)
    for pair in range(cap // 2):
        first = offset_ref[dest * cap + 2 * pair]
        second = offset_ref[dest * cap + 2 * pair + 1]
        for part in range(2):
            left = page_refs[2 * pair][0, part].astype(jnp.float32)
            right = page_refs[2 * pair + 1][0, part].astype(jnp.float32)
            left = pltpu.roll(left, lax.rem(2 * WINDOW - first, 2 * WINDOW), 1)
            right = pltpu.roll(right, WINDOW - second, 1)
            out_ref[0, pair, part] = jnp.where(lane < WINDOW, left, right).astype(out_ref.dtype)


def pack_windows(pages, table, offsets, cap):
    parts = pages.shape[1:]
    dests = table.shape[0]

    def page_spec(place):
        return pl.BlockSpec(
            (1,) + parts, lambda dest, tbl, off: (tbl[dest * cap + place], 0, 0, 0)
        )

    return pl.pallas_call(
        functools.partial(pack_kernel, cap),
        grid_spec=pltpu.PrefetchScalarGridSpec(
            num_scalar_prefetch=2,
            grid=(dests,),
            in_specs=[page_spec(place) for place in range(cap)],
            out_specs=pl.BlockSpec(
                (1, cap // 2) + parts, lambda dest, tbl, off: (dest, 0, 0, 0, 0)
            ),
        ),
        out_shape=jax.ShapeDtypeStruct((dests, cap // 2) + parts, pages.dtype),
        compiler_params=pltpu.CompilerParams(vmem_limit_bytes=VMEM_LIMIT),
        cost_estimate=SMALL,
    )(table.reshape(-1), offsets.reshape(-1), *([pages] * cap))


def attention_kernel(
    query_ref, key_before_ref, key_ref, value_before_ref, value_ref, start_ref, slot_ref, prefix_ref,
    out_ref, mixed_ref,
):
    block = pl.program_id(0)
    pairs = prefix_ref.shape[0]
    heads = query_ref.shape[1] // HEAD_SIZE
    inv_scale = 1.0 / math.sqrt(HEAD_SIZE)
    start = start_ref[...]
    slot = slot_ref[...]
    own = block * BLOCK + lax.broadcasted_iota(jnp.int32, (BLOCK, 1), 0)
    other = block * BLOCK - HALO + lax.broadcasted_iota(jnp.int32, (1, HALO + BLOCK), 1)
    local_ok = (other >= jnp.maximum(start, own - WINDOW)) & (other <= own)
    lane = lax.broadcasted_iota(jnp.int32, (1, 2 * WINDOW), 1)
    pair_of = lax.shift_right_logical(slot, 1)
    lane_low = lax.bitwise_and(slot, 1) * WINDOW
    prefix_ok = (lane >= lane_low + (own - start)) & (lane < lane_low + WINDOW)
    in_pair = [jnp.broadcast_to(pair_of == pair, (BLOCK, 2 * WINDOW)) for pair in range(pairs)]
    for head in range(heads):
        columns = slice(head * HEAD_SIZE, (head + 1) * HEAD_SIZE)
        query = query_ref[:, columns]
        keys = jnp.concatenate([key_before_ref[:, columns], key_ref[:, columns]], axis=0)
        values = jnp.concatenate([value_before_ref[:, columns], value_ref[:, columns]], axis=0)
        local = lax.dot_general(query, keys, NT, preferred_element_type=jnp.float32)
        local = jnp.where(local_ok, local * inv_scale, -1e30)
        remote = jnp.zeros((BLOCK, 2 * WINDOW), jnp.float32)
        for pair in range(0, pairs, 2):
            wide = jnp.dot(
                query,
                jnp.concatenate([prefix_ref[pair, 0, columns], prefix_ref[pair + 1, 0, columns]], axis=1),
                preferred_element_type=jnp.float32,
            )
            remote = jnp.where(in_pair[pair], wide[:, : 2 * WINDOW], remote)
            remote = jnp.where(in_pair[pair + 1], wide[:, 2 * WINDOW :], remote)
        remote = jnp.where(prefix_ok, remote * inv_scale, -1e30)
        top = jnp.maximum(
            jnp.max(local, axis=1, keepdims=True), jnp.max(remote, axis=1, keepdims=True)
        )
        local = jnp.exp(local - top)
        remote = jnp.exp(remote - top)
        total = jnp.sum(local, axis=1, keepdims=True) + jnp.sum(remote, axis=1, keepdims=True)
        remote = remote.astype(jnp.bfloat16)
        spread = jnp.concatenate(
            [jnp.where(in_pair[pair], remote, jnp.zeros_like(remote)) for pair in range(pairs)], axis=1
        )
        held = jnp.concatenate([prefix_ref[pair, 1, columns] for pair in range(pairs)], axis=1)
        mixed = jnp.dot(local.astype(jnp.bfloat16), values, preferred_element_type=jnp.float32)
        mixed = mixed + lax.dot_general(spread, held, NT, preferred_element_type=jnp.float32)
        mixed_ref[:, columns] = (mixed * (1.0 / total)).astype(jnp.bfloat16)
    width = mixed_ref.shape[1]
    for number in range(out_ref.shape[1] // width):

        @pl.when(block == number)
        def _(number=number):
            out_ref[:, number * width : (number + 1) * width] = mixed_ref[...]


def attention(query, key, value, start, slot, prefix):
    tokens, width = query.shape
    step = BLOCK // HALO
    own = pl.BlockSpec((BLOCK, width), lambda i: (i, 0))
    before = pl.BlockSpec((HALO, width), lambda i: (jnp.maximum(i * step - 1, 0), 0))
    column = pl.BlockSpec((BLOCK, 1), lambda i: (i, 0))
    wide = BLOCK, width * (tokens // BLOCK)
    return pl.pallas_call(
        attention_kernel,
        grid=(tokens // BLOCK,),
        in_specs=[
            own, before, own, before, own, column, column,
            pl.BlockSpec(prefix.shape, lambda i: (0, 0, 0, 0)),
        ],
        out_specs=pl.BlockSpec(wide, lambda i: (0, 0)),
        out_shape=jax.ShapeDtypeStruct(wide, jnp.bfloat16),
        scratch_shapes=[pltpu.VMEM((BLOCK, width), jnp.bfloat16)],
        compiler_params=pltpu.CompilerParams(vmem_limit_bytes=VMEM_LIMIT),
        cost_estimate=SMALL,
    )(query, key, key, value, value, start, slot, prefix)


def project_kernel(place_ref, *refs):
    mixed_refs, weight_refs, refs = refs[:4], refs[4:8], refs[8:]
    stream_ref, gain_ref, normed_ref, mine_ref, mixed_all_ref, resid_ref = refs
    share, (tokens, model) = mine_ref.shape[0], resid_ref.shape
    width = weight_refs[0].shape[0]
    for number, mixed_ref in enumerate(mixed_refs):
        for block in range(4):
            mixed_all_ref[number, block * share : (block + 1) * share, :] = (
                mixed_ref[:, block * width : (block + 1) * width]
            )
    squares = jnp.zeros((tokens, 128), jnp.float32)
    for first in range(0, model, LANES):
        columns = slice(first, first + LANES)
        attn = sum(
            jnp.dot(mixed_all_ref[number], weight_ref[:, columns], preferred_element_type=jnp.float32)
            for number, weight_ref in enumerate(weight_refs)
        )
        resid = (stream_ref[:, columns].astype(jnp.float32) + attn).astype(resid_ref.dtype)
        resid_ref[:, columns] = resid
        wide = resid.astype(jnp.float32)
        for part in range(0, LANES, 128):
            squares = squares + wide[:, part : part + 128] * wide[:, part : part + 128]
    scale = lax.rsqrt(jnp.sum(squares, axis=1, keepdims=True) * (1.0 / model) + 1e-06)
    gain = gain_ref[...].astype(jnp.float32)
    own = pl.multiple_of(place_ref[0] * share, share)
    mine_ref[...] = resid_ref[pl.ds(own, share), :]
    for block in range(4):
        rows = slice(block * share, (block + 1) * share)
        first = pl.multiple_of(jnp.bitwise_xor(place_ref[0], block) * share, share)
        normed_ref[pl.ds(first, share), :] = (
            resid_ref[rows, :].astype(jnp.float32) * scale[rows] * gain
        ).astype(normed_ref.dtype)


def project_and_normalise(place, mixed, weights, stream, gain):
    tokens, model = stream.shape
    smem = pl.BlockSpec(memory_space=pltpu.SMEM)
    vmem = pl.BlockSpec(memory_space=pltpu.VMEM)
    return pl.pallas_call(
        project_kernel,
        in_specs=[smem] + [vmem] * 10,
        out_specs=[vmem] * 2,
        out_shape=[
            jax.ShapeDtypeStruct((tokens, model), stream.dtype),
            jax.ShapeDtypeStruct((tokens // 4, model), stream.dtype),
        ],
        scratch_shapes=[
            pltpu.VMEM((4, tokens, weights[0].shape[0]), jnp.bfloat16),
            pltpu.VMEM((tokens, model), jnp.bfloat16),
        ],
        compiler_params=pltpu.CompilerParams(vmem_limit_bytes=VMEM_LIMIT),
        cost_estimate=SMALL,
    )(place, *mixed, *weights, stream, gain)


def ring_place(index, count):
    return jnp.where(index % 2 == 0, index // 2, count - 1 - index // 2)


def ring_index(place, count):
    place = (place + count) % count
    return jnp.where(place < count // 2, 2 * place, 2 * (count - 1 - place) + 1)


class Ring:
    def __init__(self, block, count):
        cycle = list(range(0, count, 2)) + list(range(count - 1, 0, -2))
        self.pairs = [(cycle[at], cycle[(at + 1) % count]) for at in range(count)]
        self.forward, self.backward = [block], [block]

    def step_forward(self, rows=slice(None)):
        self.forward.append(lax.ppermute(self.forward[-1][rows], "req", self.pairs))

    def step_backward(self, rows=slice(None)):
        pairs = [(there, here) for here, there in self.pairs]
        self.backward.append(lax.ppermute(self.backward[-1][rows], "req", pairs))


def step(*rings):
    for ring in rings:
        ring.step_forward()
        ring.step_backward()


def tie(rings, *others):
    last = [side[-1] for ring in rings for side in (ring.forward, ring.backward)]
    last, others = lax.optimization_barrier((last, others))
    for ring in rings:
        ring.forward[-1], ring.backward[-1], *last = last
    return others


def ring_origins(index, count, steps):
    place = ring_place(index, count)
    return jnp.stack([ring_index(place + step, count) for step in steps]).astype(jnp.int32)


def hidden_kernel(pieces, origin_ref, *refs):
    gate_refs, up_refs, refs = refs[:pieces], refs[pieces : 2 * pieces], refs[2 * pieces :]
    normed_ref, hidden_ref, gate_ref, up_ref, sems = refs
    depth, width = gate_refs[0].shape
    chunks = [slice(0, LANES), slice(LANES, width)]
    copies = [[], []]
    for part, (piece_refs, buffer) in enumerate([(gate_refs, gate_ref), (up_refs, up_ref)]):
        for number, piece_ref in enumerate(piece_refs):
            rows = pl.ds(pl.multiple_of(origin_ref[part * pieces + number] * depth, 16), depth)
            for chunk, columns in enumerate(chunks):
                copies[chunk].append(
                    pltpu.make_async_copy(
                        piece_ref.at[:, columns],
                        buffer.at[rows, columns],
                        sems.at[chunk, part * pieces + number],
                    )
                )
    for chunk in copies:
        for copy in chunk:
            copy.start()
    for first in range(0, width, LANES):
        columns = slice(first, min(first + LANES, width))
        if first in (0, LANES):
            for copy in copies[first // LANES]:
                copy.wait()
        gate = jnp.dot(normed_ref[...], gate_ref[:, columns], preferred_element_type=jnp.float32)
        up = jnp.dot(normed_ref[...], up_ref[:, columns], preferred_element_type=jnp.float32)
        hidden_ref[:, columns] = (gate / (1.0 + jnp.exp(-gate)) * up).astype(jnp.bfloat16)


def hidden_units(origins, gate_pieces, up_pieces, normed):
    width = gate_pieces[0].shape[1]
    tokens, model = normed.shape
    count = len(gate_pieces)
    pieces = gate_pieces + up_pieces
    smem = pl.BlockSpec(memory_space=pltpu.SMEM)
    vmem = pl.BlockSpec(memory_space=pltpu.VMEM)
    anywhere = pl.BlockSpec(memory_space=pl.ANY)
    return pl.pallas_call(
        functools.partial(hidden_kernel, count),
        in_specs=[smem] + [anywhere] * len(pieces) + [vmem],
        out_specs=vmem,
        out_shape=jax.ShapeDtypeStruct((tokens, width), jnp.bfloat16),
        scratch_shapes=[
            pltpu.VMEM((model, width), jnp.bfloat16),
            pltpu.VMEM((model, width), jnp.bfloat16),
            pltpu.SemaphoreType.DMA((2, len(pieces))),
        ],
        compiler_params=pltpu.CompilerParams(vmem_limit_bytes=VMEM_LIMIT),
        cost_estimate=SMALL,
    )(origins, *pieces, normed)


def down_kernel(pieces, hidden_ref, *refs):
    piece_refs, out_refs = refs[:pieces], refs[pieces:]
    hidden = hidden_ref[...]
    blocks = [piece_ref[...] for piece_ref in piece_refs]
    depth = blocks[0].shape[0]
    if blocks[-1].shape[0] < depth:
        blocks[-2:] = [jnp.concatenate(blocks[-2:], axis=0)]
    for number, block in enumerate(blocks):
        columns = slice(number * depth, (number + 1) * depth)
        part = lax.dot_general(hidden, block, NT, preferred_element_type=jnp.float32)
        first = 0
        for out_ref in out_refs:
            rows = out_ref.shape[0]
            out_ref[:, columns] = part[first : first + rows].astype(out_ref.dtype)
            first += rows


def down_sums(pieces, hidden, cost=SMALL):
    tokens = hidden.shape[0]
    columns = sum(piece.shape[0] for piece in pieces)
    vmem = pl.BlockSpec(memory_space=pltpu.VMEM)
    return pl.pallas_call(
        functools.partial(down_kernel, len(pieces)),
        in_specs=[vmem] * (1 + len(pieces)),
        out_specs=[vmem] * 4,
        out_shape=[jax.ShapeDtypeStruct((tokens // 4, columns), jnp.bfloat16)] * 4,
        compiler_params=pltpu.CompilerParams(vmem_limit_bytes=VMEM_LIMIT),
        cost_estimate=cost,
    )(hidden, *pieces)


def place_kernel(groups, depth, origin_ref, resid_ref, *refs):
    term_refs, (out_ref, sum_ref) = refs[:-2], refs[-2:]
    rows, model = out_ref.shape
    sum_ref[...] = jnp.zeros_like(sum_ref)
    number, span = 0, 3 * 128
    for count, parts in groups:
        terms, term_refs = term_refs[:parts], term_refs[parts:]
        total = sum(term_ref[...].astype(jnp.float32) for term_ref in terms)
        for entry in range(count):
            first = origin_ref[number] * depth
            block = total[:, entry * depth : (entry + 1) * depth]
            block = jnp.concatenate([block, jnp.zeros((rows, span - depth), jnp.float32)], axis=1)
            block = pltpu.roll(block, lax.rem(first, 128), 1)
            lanes = pl.ds(pl.multiple_of(lax.div(first, 128) * 128, 128), span)
            sum_ref[:, lanes] += block
            number += 1
    out_ref[...] = (resid_ref[...].astype(jnp.float32) + sum_ref[:, :model]).astype(out_ref.dtype)


def place_and_add(origins, resid, groups, depth):
    sizes = [(terms[0].shape[1] // depth, len(terms)) for terms in groups]
    smem = pl.BlockSpec(memory_space=pltpu.SMEM)
    vmem = pl.BlockSpec(memory_space=pltpu.VMEM)
    terms = [term for group in groups for term in group]
    rows, model = resid.shape
    return pl.pallas_call(
        functools.partial(place_kernel, sizes, depth),
        in_specs=[smem] + [vmem] * (1 + len(terms)),
        out_specs=vmem,
        out_shape=jax.ShapeDtypeStruct(resid.shape, resid.dtype),
        scratch_shapes=[pltpu.VMEM((rows, model + 128), jnp.float32)],
        compiler_params=pltpu.CompilerParams(vmem_limit_bytes=VMEM_LIMIT),
        cost_estimate=SMALL,
    )(origins, resid, *terms)


def core_swap(array):
    return lax.ppermute(array, "mdl", [(0, 1), (1, 0), (2, 3), (3, 2)])


def chip_swap(array):
    return lax.ppermute(array, "mdl", [(0, 2), (2, 0), (1, 3), (3, 1)])


def gather_model(array):
    far = chip_swap(array)
    return [array, core_swap(array), far, core_swap(far)]


def sum_on_chip(keep, send):
    wide = jnp.float32
    return (keep.astype(wide) + core_swap(send).astype(wide)).astype(keep.dtype)


def sum_here(own, other, across):
    wide = jnp.float32
    return own.astype(wide) + core_swap(other).astype(wide) + across.astype(wide)


def normalise(resid, gain):
    wide = resid.astype(jnp.float32)
    mean_sq = jnp.mean(wide * wide, axis=1, keepdims=True)
    return (wide * lax.rsqrt(mean_sq + 1e-06) * gain.astype(jnp.float32)[None, :]).astype(jnp.bfloat16)


def per_device(
    stream,
    attention_projection_weight,
    head_output_weight,
    adapter_down_maps,
    adapter_up_maps,
    tenant_adapter_scale,
    feedforward_norm_gain,
    feedforward_weight,
    prefix_cache_store,
    token_adapter_index,
    request_token_lengths,
    request_tenant_index,
    last_page_holder,
    holder_page_slot,
    page_filled_rows,
):
    tok_count, model_width = stream.shape
    req_per_dev = request_token_lengths.shape[1]
    rank_total_width = adapter_down_maps.shape[2]
    adapter_number = adapter_up_maps.shape[2] // rank_total_width
    req_devices = lax.axis_size("req")
    req_index = lax.axis_index("req")
    mdl_index = lax.axis_index("mdl")
    row_share = tok_count // lax.axis_size("mdl")
    cap_slots = max(2, (req_per_dev + req_devices - 1) // req_devices + 1)
    cap_slots += cap_slots % 2

    order_ids = jnp.arange(req_per_dev, dtype=jnp.int32)
    owner_table = last_page_holder[:, 0].reshape(req_devices, req_per_dev)
    slot_table = holder_page_slot.reshape(req_devices, req_per_dev)
    offset_table = page_filled_rows.reshape(req_devices, req_per_dev) - WINDOW
    owned = (owner_table == req_index).astype(jnp.int32)
    earlier_one = (order_ids[:, None] > order_ids[None, :]).astype(jnp.int32)
    owned_rank = jnp.sum(owned[:, None, :] * earlier_one[None], axis=2)
    picked = owned[:, None, :] * (
        owned_rank[:, None, :] == jnp.arange(cap_slots, dtype=jnp.int32)[None, :, None]
    ).astype(jnp.int32)
    send_slot = jnp.sum(picked * slot_table[:, None, :], axis=2)
    send_offset = jnp.sum(picked * offset_table[:, None, :], axis=2)
    packed = pack_windows(prefix_cache_store, send_slot, send_offset, cap_slots)
    rows_held = feedforward_weight.shape[1]
    ringed = (lax.axis_size("mdl"), tok_count // BLOCK, req_devices, rows_held % 32) == (4, 4, 8, 0)
    if ringed:
        half = req_devices // 2
        near_steps = [-k for k in range(3)] + [1, 2]
        far_steps = [sign * k for k in range(3, half) for sign in (-1, 1)] + [half]
        gate_steps = [-k for k in range(half + 1)] + list(range(1, half))
        up_steps = [-k for k in range(half)] + list(range(1, half + 1))
        origins = ring_origins(req_index, req_devices, gate_steps + up_steps)
        down_origins = ring_origins(req_index, req_devices, near_steps + far_steps)
        gate, up = Ring(feedforward_weight[0], req_devices), Ring(feedforward_weight[1], req_devices)
        step(gate, up)
        (packed,) = tie([gate, up], packed)
        step(gate, up)
    arrived = lax.all_to_all(packed, "req", split_axis=0, concat_axis=0, tiled=True)

    projected_rows = [
        lax.dot_general(
            stream, attention_projection_weight[k], NT, preferred_element_type=jnp.float32
        )
        for k in range(3)
    ]
    holder_count = adapter_down_maps.shape[0]
    holder_rank_rows = jnp.einsum(
        "qf,kfn->qkn", stream, adapter_down_maps, preferred_element_type=jnp.float32
    )
    held_onehot = (
        token_adapter_index[:, None]
        == (mdl_index * holder_count + jnp.arange(holder_count, dtype=jnp.int32))[None, :]
    )
    rank_part = jnp.sum(holder_rank_rows * held_onehot.astype(jnp.float32)[:, :, None], axis=1)
    rank_feat = lax.psum(rank_part.astype(jnp.bfloat16), "mdl")
    all_onehot = (
        token_adapter_index[:, None] == jnp.arange(adapter_number, dtype=jnp.int32)[None, :]
    )
    broadcast_result = (
        all_onehot.astype(jnp.bfloat16)[:, :, None] * rank_feat[:, None, :]
    ).reshape(tok_count, adapter_number * rank_total_width)
    lora_query = lax.dot_general(
        broadcast_result, adapter_up_maps[0], NT, preferred_element_type=jnp.float32
    )
    lora_value = lax.dot_general(
        broadcast_result, adapter_up_maps[1], NT, preferred_element_type=jnp.float32
    )

    positions = jnp.arange(tok_count, dtype=jnp.int32)
    lengths_row = request_token_lengths[0]
    ends = jnp.sum(
        jnp.where(order_ids[:, None] >= order_ids[None, :], lengths_row[None, :], 0), axis=1
    )
    starts = ends - lengths_row
    member = (positions[:, None] >= starts[None, :]) & (positions[:, None] < ends[None, :])
    member_int = member.astype(jnp.int32)
    start_of = jnp.sum(member_int * starts[None, :], axis=1, keepdims=True)
    my_owner = lax.dynamic_slice_in_dim(owner_table, req_index, 1, 0)[0]
    earlier = (my_owner[:, None] == my_owner[None, :]).astype(jnp.int32) * earlier_one
    slot_in = my_owner * cap_slots + jnp.sum(earlier, axis=1)
    slot_of = jnp.sum(member_int * slot_in[None, :], axis=1, keepdims=True)
    tenant_hot = (
        request_tenant_index[:, None]
        == jnp.arange(tenant_adapter_scale.shape[0], dtype=jnp.int32)[None, :]
    ).astype(jnp.float32)
    request_scale = jnp.sum(tenant_hot * tenant_adapter_scale[None, :], axis=1)
    per_token_scale = jnp.sum(member.astype(jnp.float32) * request_scale[None, :], axis=1)[:, None]
    query_rows = (projected_rows[0] + per_token_scale * lora_query).astype(jnp.bfloat16)
    key_rows = projected_rows[1].astype(jnp.bfloat16)
    value_rows = (projected_rows[2] + per_token_scale * lora_value).astype(jnp.bfloat16)

    prefix = arrived.reshape((-1,) + arrived.shape[2:])
    blocks = tok_count // BLOCK
    if ringed:
        prefix, query_rows, key_rows, value_rows, *weights = tie(
            [gate, up], prefix, query_rows, key_rows, value_rows, *gather_model(head_output_weight)
        )
        step(gate, up)
        mixed = attention(query_rows, key_rows, value_rows, start_of, slot_of, prefix)
        (mixed,) = tie([gate, up], mixed)
        gate.step_forward()
        up.step_backward()
        (down_block,) = tie([gate, up], feedforward_weight[2])
        down = Ring(down_block, req_devices)
        step(down)
        normed, resid = project_and_normalise(
            mdl_index.reshape(1).astype(jnp.int32), gather_model(mixed), weights, stream,
            feedforward_norm_gain.reshape(1, model_width),
        )
        (normed,) = tie([down], normed)
        step(down)
        hidden = hidden_units(
            origins, gate.forward + gate.backward[1:], up.forward + up.backward[1:], normed
        )
        (hidden,) = tie([down], hidden)
        for _ in range(3, half):
            step(down)
        near_pieces = down.forward[:3] + down.backward[1:3]
        far_pieces = [side[k] for k in range(3, half) for side in (down.forward, down.backward)]
        down.step_forward(slice(0, rows_held // 2))
        down.step_backward(slice(rows_held // 2, rows_held))
        far_pieces += [down.forward[-1], down.backward[-1]]
        own, other, keep, send = down_sums(near_pieces, hidden)
        across = chip_swap(sum_on_chip(keep, send))
        near_terms = own, other
        far_cost = pl.CostEstimate(flops=1 << 33, bytes_accessed=0, transcendentals=0)
        own, other, keep, send = down_sums(far_pieces, hidden, far_cost)
        keep, near_sum = lax.optimization_barrier((keep, sum_here(*near_terms, across)))
        part = sum_on_chip(keep, send)
        groups = [near_sum], [own, core_swap(other), chip_swap(part)]
        return place_and_add(down_origins, resid, groups, rows_held)

    mixed = attention(query_rows, key_rows, value_rows, start_of, slot_of, prefix)
    mixed = jnp.concatenate(jnp.split(mixed, blocks, axis=1), axis=0)
    attn_part = jnp.dot(mixed, head_output_weight, preferred_element_type=jnp.float32).astype(jnp.bfloat16)
    attn_full = lax.psum(attn_part, "mdl").astype(jnp.float32)
    resid = (stream.astype(jnp.float32) + attn_full).astype(jnp.bfloat16)
    normed = normalise(resid, feedforward_norm_gain)
    resid_mine = lax.dynamic_slice_in_dim(resid, mdl_index * row_share, row_share, 0)
    full_mlp = lax.all_gather(feedforward_weight, "req", axis=1, tiled=True)
    gate_part = jnp.dot(normed, full_mlp[0], preferred_element_type=jnp.float32)
    up_part = jnp.dot(normed, full_mlp[1], preferred_element_type=jnp.float32)
    hidden = (jax.nn.silu(gate_part) * up_part).astype(jnp.bfloat16)
    mlp_part = lax.dot_general(
        hidden, full_mlp[2], NT, preferred_element_type=jnp.float32
    ).astype(jnp.bfloat16)
    mlp_mine = lax.psum_scatter(mlp_part, "mdl", scatter_dimension=0, tiled=True)
    return (resid_mine.astype(jnp.float32) + mlp_mine.astype(jnp.float32)).astype(jnp.bfloat16)


def solution(mesh):
    return jax.shard_map(
        per_device,
        mesh=mesh,
        in_specs=(
            P("req", None),
            P(None, "mdl", None),
            P("mdl", None),
            P("mdl", None, None),
            P(None, "mdl", None),
            P(),
            P(),
            P(None, "req", "mdl"),
            P("req", None, "mdl", None),
            P("req"),
            P("req", None),
            P("req"),
            P(),
            P(),
            P(),
        ),
        out_specs=P(("req", "mdl"), None),
        check_vma=False,
    )
```

profile of v0, /device:TPU:0, one launch (start us, length us, event | category | flops | bytes accessed | tf_op | source)
XLA Modules:
  0.0 262.1 jit_solution(2811215112134056060)
XLA Ops:
  1.6 3.1 %collective-permute-start = (bf16[224,1216]{1,0:T(8,128)(2,1)S(1)}, bf16[224,1216]{1,0:T(8,128)(2,1)S(1)}, u32[]{:S(2)}, u32[]{:S(2)}) collective-permute-start(bf16[224,1216]{1,0:T(8,128)(2,1)S(1)} %get-tuple-element.100.refs_0_), channel_id=1, source_target_pairs={{0,8},{8,16},{16,24},{24,28},{28,20},{20,12},{12,4},{4,0},{1,9},{9... | collective-permute-start | bytes 1634312 | tf_op jit(solution)/shard_map/ppermute | solution.py:211
  4.7 2.0 collective-permute-start.2
  8.9 7.1 %shard_map.145 = bf16[8,2,2,448,128]{4,3,2,1,0:T(8,128)(2,1)S(1)} custom-call(s32[32]{0:T(128)S(1)} %reshape.124.table_ref, s32[32]{0:T(128)S(1)} %reshape.125.offset_ref, bf16[32,2,448,128]{3,2,1,0:T(8,128)(2,1)} %refs_3_.1, bf16[32,2,448,128]{3,2,1,0:T(8,128)(2,1)} %refs_3_.1, bf16[32,2,448,128]{3,2,1,0:T(8,128)(2,1)} %refs_3_.1, ...), custom_call_target="tpu_custom_call" | custom-call | tf_op jit(solution)/shard_map/pallas_call | solution.py:45
  16.0 1.8 copy-done.2
  18.5 2.3 collective-permute-done.1.refs_5_
  20.7 9.3 %collective-permute-done.2.refs_9_ = bf16[224,1216]{1,0:T(8,128)(2,1)} collective-permute-done((bf16[224,1216]{1,0:T(8,128)(2,1)S(1)}, bf16[224,1216]{1,0:T(8,128)(2,1)}, u32[]{:S(2)}, u32[]{:S(2)}) %collective-permute-start.2) | collective-permute-done | bytes 544800 | tf_op jit(solution)/shard_map/ppermute | solution.py:211
  31.5 4.8 %all-to-all-start = ((bf16[8,2,2,448,128]{4,3,2,1,0:T(8,128)(2,1)}), bf16[8,2,2,448,128]{4,3,2,1,0:T(8,128)(2,1)}, u32[]{:S(2)}, u32[]{:S(2)}) async-start(bf16[8,2,2,448,128]{4,3,2,1,0:T(8,128)(2,1)} %copy-done.2), calls=%async_computation | async-start | bytes 7340032 | tf_op jit(solution)/shard_map/all_to_all | solution.py:441
  38.1 2.7 %fusion.24 = f32[768,256]{0,1:S(1)} fusion(bf16[768,1792]{1,0:T(8,128)(2,1)} %refs_8_.1, bf16[1792,256]{0,1:T(8,128)(2,1)S(1)} %bitcast.62), kind=kOutput, calls=%fused_computation.55 | convolution fusion | flops 704643072 | bytes 4456448
  40.8 40.9 %psum.7 = bf16[768,16]{0,1:T(8,128)(2,1)S(1)} all-reduce(bf16[768,16]{0,1:T(8,128)(2,1)S(1)} %multiply_reduce_fusion), channel_id=1, replica_groups=mesh['req'=8,'mdl'=4] {'mdl'}, use_global_device_ids=true, to_apply=%region_7.8 | all-reduce | flops 12288 | bytes 49152 | tf_op jit(solution)/shard_map/psum | solution.py:458
  82.2 4.0 %fusion.4 = f32[768,448]{1,0:T(8,128)S(1)} fusion(bf16[768,1792]{1,0:T(8,128)(2,1)} %refs_8_.1, bf16[3,448,1792]{2,1,0:T(8,128)(2,1)} %param.16), kind=kOutput, calls=%fused_computation.4 | convolution fusion | flops 1233125376 | bytes 5734400 | tf_op jit(solution)/shard_map/dot_general | solution.py:444
  86.2 2.1 collective-permute-start.4
  88.3 2.0 add_convert_fusion.1.query_ref
  90.3 3.0 %fusion = f32[768,448]{1,0:T(8,128)S(1)} fusion(bf16[768,1792]{1,0:T(8,128)(2,1)S(1)} %copy-done.18, bf16[3,448,1792]{2,1,0:T(8,128)(2,1)} %param.16), kind=kOutput, calls=%fused_computation | convolution fusion | flops 1233125376 | bytes 5734400 | tf_op jit(solution)/shard_map/dot_general | solution.py:444
  93.4 2.0 collective-permute-start.6
  95.4 14.2 %collective-permute-done.4.refs_2_ = bf16[224,1216]{1,0:T(8,128)(2,1)} collective-permute-done((bf16[224,1216]{1,0:T(8,128)(2,1)S(1)}, bf16[224,1216]{1,0:T(8,128)(2,1)}, u32[]{:S(2)}, u32[]{:S(2)}) %collective-permute-start.4) | collective-permute-done | bytes 544800 | tf_op jit(solution)/shard_map/ppermute | solution.py:211
  110.8 3.9 %fusion.9.key_before_ref.key_ref = bf16[768,448]{1,0:T(8,128)(2,1)S(1)} fusion(bf16[768,1792]{1,0:T(8,128)(2,1)} %refs_8_.1, bf16[3,448,1792]{2,1,0:T(8,128)(2,1)} %param.16), kind=kOutput, calls=%fused_computation.11 | convolution fusion | flops 1233469440 | bytes 5046272 | tf_op jit(solution)/shard_map/dot_general | solution.py:444
  114.6 12.3 %collective-permute-done.5.refs_6_ = bf16[224,1216]{1,0:T(8,128)(2,1)} collective-permute-done((bf16[224,1216]{1,0:T(8,128)(2,1)}, bf16[224,1216]{1,0:T(8,128)(2,1)}, u32[]{:S(2)}, u32[]{:S(2)}) %collective-permute-start.5) | collective-permute-done | bytes 544800 | tf_op jit(solution)/shard_map/ppermute | solution.py:215
  127.0 15.4 %collective-permute-done.7.refs_13_ = bf16[224,1216]{1,0:T(8,128)(2,1)S(1)} collective-permute-done((bf16[224,1216]{1,0:T(8,128)(2,1)}, bf16[224,1216]{1,0:T(8,128)(2,1)S(1)}, u32[]{:S(2)}, u32[]{:S(2)}) %collective-permute-start.7) | collective-permute-done | bytes 544800 | tf_op jit(solution)/shard_map/ppermute | solution.py:215
  142.3 2.6 %collective-permute-start.11 = (bf16[224,1216]{1,0:T(8,128)(2,1)}, bf16[224,1216]{1,0:T(8,128)(2,1)S(1)}, u32[]{:S(2)}, u32[]{:S(2)}) collective-permute-start(bf16[224,1216]{1,0:T(8,128)(2,1)} %collective-permute-done.4.refs_2_), channel_id=1, source_target_pairs={{0,8},{8,16},{16,24},{24,28},{28,20},{20,12},{12,4},{4,0},{1,9},{9... | collective-permute-start | bytes 1634312 | tf_op jit(solution)/shard_map/ppermute | solution.py:211
  145.0 2.0 collective-permute-start.13
  148.8 15.7 %shard_map.146.refs_0_ = bf16[192,1792]{1,0:T(8,128)(2,1)S(1)} custom-call(bf16[768,448]{1,0:T(8,128)(2,1)S(1)} %copy-done.9, bf16[768,448]{1,0:T(8,128)(2,1)S(1)} %fusion.9.key_before_ref.key_ref, bf16[768,448]{1,0:T(8,128)(2,1)S(1)} %fusion.9.key_before_ref.key_ref, bf16[768,448]{1,0:T(8,128)(2,1)S(1)} %add_convert_fusion.value_before_ref.value_ref, ...), custom_call_target="tpu_custom_call" | custom-call | tf_op jit(solution)/shard_map/pallas_call | solution.py:125
  165.4 4.0 %collective-permute-done.13.refs_11_ = bf16[224,1216]{1,0:T(8,128)(2,1)S(1)} collective-permute-done((bf16[224,1216]{1,0:T(8,128)(2,1)}, bf16[224,1216]{1,0:T(8,128)(2,1)S(1)}, u32[]{:S(2)}, u32[]{:S(2)}) %collective-permute-start.13) | collective-permute-done | bytes 544800 | tf_op jit(solution)/shard_map/ppermute | solution.py:211
  169.4 2.1 collective-permute-done.14.refs_14_
  175.0 12.0 %collective-permute-done.16.refs_2_ = bf16[192,1792]{1,0:T(8,128)(2,1)S(1)} collective-permute-done((bf16[192,1792]{1,0:T(8,128)(2,1)S(1)}, bf16[192,1792]{1,0:T(8,128)(2,1)S(1)}, u32[]{:S(2)}, u32[]{:S(2)}) %collective-permute-start.16) | collective-permute-done | bytes 688160 | tf_op jit(solution)/shard_map/ppermute | solution.py:362
  189.9 11.7 %shard_map.147 = (bf16[768,1792]{1,0:T(8,128)(2,1)}, bf16[192,1792]{1,0:T(8,128)(2,1)S(1)}) custom-call(s32[1]{0:T(128)} %bitcast.8.place_ref, bf16[192,1792]{1,0:T(8,128)(2,1)S(1)} %shard_map.146.refs_0_, bf16[192,1792]{1,0:T(8,128)(2,1)S(1)} %collective-permute-done.15.refs_1_, bf16[192,1792]{1,0:T(8,128)(2,1)S(1)} %collective-permute-done.16.refs_2_, ...), custom_call_target="tpu_custom_call" | custom-call | tf_op jit(solution)/shard_map/pallas_call | solution.py:178
  210.5 12.2 %shard_map.148.hidden_ref = bf16[768,1216]{1,0:T(8,128)(2,1)} custom-call(s32[16]{0:T(128)S(1)} %stack.58.origin_ref, bf16[224,1216]{1,0:T(8,128)(2,1)S(1)} %copy-done.5, bf16[224,1216]{1,0:T(8,128)(2,1)S(1)} %copy-done.11, bf16[224,1216]{1,0:T(8,128)(2,1)} %collective-permute-done.4.refs_2_, bf16[224,1216]{1,0:T(8,128)(2,1)S(1)} %copy-done.13, ...), custom_call_target="tpu_custom_call" | custom-call | tf_op jit(solution)/shard_map/pallas_call | solution.py:275
  224.9 4.8 %shard_map.150 = (bf16[192,1120]{1,0:T(8,128)(2,1)S(1)}, bf16[192,1120]{1,0:T(8,128)(2,1)S(1)}, bf16[192,1120]{1,0:T(8,128)(2,1)S(1)}, bf16[192,1120]{1,0:T(8,128)(2,1)S(1)}) custom-call(bf16[768,1216]{1,0:T(8,128)(2,1)} %shard_map.148.hidden_ref, bf16[224,1216]{1,0:T(8,128)(2,1)S(1)} %get-tuple-element.73.refs_0_, ...), custom_call_target="tpu_custom_call" | custom-call | tf_op jit(solution)/shard_map/pallas_call | solution.py:311
  230.2 6.5 %collective-permute-done.24.refs_0_ = bf16[224,1216]{1,0:T(8,128)(2,1)S(1)} collective-permute-done((bf16[224,1216]{1,0:T(8,128)(2,1)}, bf16[224,1216]{1,0:T(8,128)(2,1)S(1)}, u32[]{:S(2)}, u32[]{:S(2)}) %collective-permute-start.24) | collective-permute-done | bytes 544800 | tf_op jit(solution)/shard_map/ppermute | solution.py:211
  240.6 2.9 %collective-permute-done.26.refs_2_ = bf16[112,1216]{1,0:T(8,128)(2,1)S(1)} collective-permute-done((bf16[112,1216]{1,0:T(8,128)(2,1)S(1)}, bf16[112,1216]{1,0:T(8,128)(2,1)S(1)}, u32[]{:S(2)}, u32[]{:S(2)}) %collective-permute-start.26) | collective-permute-done | bytes 272416 | tf_op jit(solution)/shard_map/ppermute | solution.py:211
  244.2 2.4 shard_map.149
  251.1 7.7 %collective-permute-done.33.refs_3_ = bf16[192,672]{1,0:T(8,128)(2,1)} collective-permute-done((bf16[192,672]{1,0:T(8,128)(2,1)}, bf16[192,672]{1,0:T(8,128)(2,1)}, u32[]{:S(2)}, u32[]{:S(2)}) %collective-permute-start.33) | collective-permute-done | bytes 258080 | tf_op jit(solution)/shard_map/ppermute | solution.py:362
  258.8 3.3 %shard_map.151 = bf16[192,1792]{1,0:T(8,128)(2,1)} custom-call(s32[8]{0:T(128)S(1)} %stack.56.origin_ref, bf16[192,1792]{1,0:T(8,128)(2,1)S(1)} %get-tuple-element.68.resid_ref, f32[192,1120]{1,0:T(8,128)S(1)} %convert_add_fusion.refs_0_, bf16[192,672]{1,0:T(8,128)(2,1)S(1)} %get-tuple-element.91.refs_1_, ...), custom_call_target="tpu_custom_call" | custom-call | tf_op jit(solution)/shard_map/pallas_call | solution.py:346
  (154 shorter events, 38.8 us)
Async XLA Ops:
  1.6 16.8 %collective-permute-start = (bf16[224,1216]{1,0:T(8,128)(2,1)S(1)}, bf16[224,1216]{1,0:T(8,128)(2,1)S(1)}, u32[]{:S(2)}, u32[]{:S(2)}) collective-permute-start(bf16[224,1216]{1,0:T(8,128)(2,1)S(1)} %get-tuple-element.100.refs_0_), channel_id=1, source_target_pairs={{0,8},{8,16},{16,24},{24,28},{28,20},{20,12},{12,4},{4,0},{1,9},{9... | collective-permute-start | bytes 1634312 | tf_op jit(solution)/shard_map/ppermute | solution.py:211
  4.7 16.0 %collective-permute-start.1 = (bf16[224,1216]{1,0:T(8,128)(2,1)S(1)}, bf16[224,1216]{1,0:T(8,128)(2,1)}, u32[]{:S(2)}, u32[]{:S(2)}) collective-permute-start(bf16[224,1216]{1,0:T(8,128)(2,1)S(1)} %get-tuple-element.100.refs_0_), channel_id=1, source_target_pairs={{8,0},{16,8},{24,16},{28,24},{20,28},{12,20},{4,12},{0,4},{9,1},{1... | collective-permute-start | bytes 1634312 | tf_op jit(solution)/shard_map/ppermute | solution.py:215
  4.7 25.3 %collective-permute-start.2 = (bf16[224,1216]{1,0:T(8,128)(2,1)S(1)}, bf16[224,1216]{1,0:T(8,128)(2,1)}, u32[]{:S(2)}, u32[]{:S(2)}) collective-permute-start(bf16[224,1216]{1,0:T(8,128)(2,1)S(1)} %get-tuple-element.101.refs_8_), channel_id=1, source_target_pairs={{0,8},{8,16},{16,24},{24,28},{28,20},{20,12},{12,4},{4,0},{1,9},{9... | collective-permute-start | bytes 1634312 | tf_op jit(solution)/shard_map/ppermute | solution.py:211
  6.7 24.8 %collective-permute-start.3 = (bf16[224,1216]{1,0:T(8,128)(2,1)S(1)}, bf16[224,1216]{1,0:T(8,128)(2,1)}, u32[]{:S(2)}, u32[]{:S(2)}) collective-permute-start(bf16[224,1216]{1,0:T(8,128)(2,1)S(1)} %get-tuple-element.101.refs_8_), channel_id=1, source_target_pairs={{8,0},{16,8},{24,16},{28,24},{20,28},{12,20},{4,12},{0,4},{9,1},{1... | collective-permute-start | bytes 1634312 | tf_op jit(solution)/shard_map/ppermute | solution.py:215
  31.5 110.8 %all-to-all-start = ((bf16[8,2,2,448,128]{4,3,2,1,0:T(8,128)(2,1)}), bf16[8,2,2,448,128]{4,3,2,1,0:T(8,128)(2,1)}, u32[]{:S(2)}, u32[]{:S(2)}) async-start(bf16[8,2,2,448,128]{4,3,2,1,0:T(8,128)(2,1)} %copy-done.2), calls=%async_computation | async-start | bytes 7340032 | tf_op jit(solution)/shard_map/all_to_all | solution.py:441
  36.4 106.0 %collective-permute-start.8 = (bf16[448,1792]{1,0:T(8,128)(2,1)}, bf16[448,1792]{1,0:T(8,128)(2,1)}, u32[]{:S(2)}, u32[]{:S(2)}) collective-permute-start(bf16[448,1792]{1,0:T(8,128)(2,1)} %refs_4_), channel_id=1, source_target_pairs={{0,1},{1,0},{2,3},{3,2},{4,5},{5,4},{6,7},{7,6},{8,9},{9,8},{10,11... | collective-permute-start | bytes 4816904 | tf_op jit(solution)/shard_map/ppermute | solution.py:358
  36.4 51.9 %collective-permute-start.9 = (bf16[448,1792]{1,0:T(8,128)(2,1)}, bf16[448,1792]{1,0:T(8,128)(2,1)}, u32[]{:S(2)}, u32[]{:S(2)}) collective-permute-start(bf16[448,1792]{1,0:T(8,128)(2,1)} %refs_4_), channel_id=1, source_target_pairs={{0,2},{2,0},{1,3},{3,1},{4,6},{6,4},{5,7},{7,5},{8,10},{10,8},{9,1... | collective-permute-start | bytes 4816904 | tf_op jit(solution)/shard_map/ppermute | solution.py:362
  86.2 23.5 %collective-permute-start.4 = (bf16[224,1216]{1,0:T(8,128)(2,1)S(1)}, bf16[224,1216]{1,0:T(8,128)(2,1)}, u32[]{:S(2)}, u32[]{:S(2)}) collective-permute-start(bf16[224,1216]{1,0:T(8,128)(2,1)S(1)} %collective-permute-done.refs_1_), channel_id=1, source_target_pairs={{0,8},{8,16},{16,24},{24,28},{28,20},{20,12},{12,4},{4,0},{1,9},{9... | collective-permute-start | bytes 1634312 | tf_op jit(solution)/shard_map/ppermute | solution.py:211
  88.3 54.1 %collective-permute-start.10 = (bf16[448,1792]{1,0:T(8,128)(2,1)}, bf16[448,1792]{1,0:T(8,128)(2,1)}, u32[]{:S(2)}, u32[]{:S(2)}) collective-permute-start(bf16[448,1792]{1,0:T(8,128)(2,1)} %collective-permute-done.9.refs_6_), channel_id=1, source_target_pairs={{0,1},{1,0},{2,3},{3,2},{4,5},{5,4},{6,7},{7,6},{8,9},{9,8},{10,11... | collective-permute-start | bytes 4816904 | tf_op jit(solution)/shard_map/ppermute | solution.py:358
  93.4 33.6 %collective-permute-start.5 = (bf16[224,1216]{1,0:T(8,128)(2,1)}, bf16[224,1216]{1,0:T(8,128)(2,1)}, u32[]{:S(2)}, u32[]{:S(2)}) collective-permute-start(bf16[224,1216]{1,0:T(8,128)(2,1)} %collective-permute-done.1.refs_5_), channel_id=1, source_target_pairs={{8,0},{16,8},{24,16},{28,24},{20,28},{12,20},{4,12},{0,4},{9,1},{1... | collective-permute-start | bytes 1634312 | tf_op jit(solution)/shard_map/ppermute | solution.py:215
  93.4 33.5 %collective-permute-start.6 = (bf16[224,1216]{1,0:T(8,128)(2,1)}, bf16[224,1216]{1,0:T(8,128)(2,1)}, u32[]{:S(2)}, u32[]{:S(2)}) collective-permute-start(bf16[224,1216]{1,0:T(8,128)(2,1)} %collective-permute-done.2.refs_9_), channel_id=1, source_target_pairs={{0,8},{8,16},{16,24},{24,28},{28,20},{20,12},{12,4},{4,0},{1,9},{9... | collective-permute-start | bytes 1634312 | tf_op jit(solution)/shard_map/ppermute | solution.py:211
  109.7 32.6 %collective-permute-start.7 = (bf16[224,1216]{1,0:T(8,128)(2,1)}, bf16[224,1216]{1,0:T(8,128)(2,1)S(1)}, u32[]{:S(2)}, u32[]{:S(2)}) collective-permute-start(bf16[224,1216]{1,0:T(8,128)(2,1)} %collective-permute-done.3.refs_12_), channel_id=1, source_target_pairs={{8,0},{16,8},{24,16},{28,24},{20,28},{12,20},{4,12},{0,4},{9,1},{1... | collective-permute-start | bytes 1634312 | tf_op jit(solution)/shard_map/ppermute | solution.py:215
  142.3 22.2 %collective-permute-start.11 = (bf16[224,1216]{1,0:T(8,128)(2,1)}, bf16[224,1216]{1,0:T(8,128)(2,1)S(1)}, u32[]{:S(2)}, u32[]{:S(2)}) collective-permute-start(bf16[224,1216]{1,0:T(8,128)(2,1)} %collective-permute-done.4.refs_2_), channel_id=1, source_target_pairs={{0,8},{8,16},{16,24},{24,28},{28,20},{20,12},{12,4},{4,0},{1,9},{9... | collective-permute-start | bytes 1634312 | tf_op jit(solution)/shard_map/ppermute | solution.py:211
  145.0 19.6 %collective-permute-start.12 = (bf16[224,1216]{1,0:T(8,128)(2,1)}, bf16[224,1216]{1,0:T(8,128)(2,1)S(1)}, u32[]{:S(2)}, u32[]{:S(2)}) collective-permute-start(bf16[224,1216]{1,0:T(8,128)(2,1)} %collective-permute-done.5.refs_6_), channel_id=1, source_target_pairs={{8,0},{16,8},{24,16},{28,24},{20,28},{12,20},{4,12},{0,4},{9,1},{1... | collective-permute-start | bytes 1634312 | tf_op jit(solution)/shard_map/ppermute | solution.py:215
  145.0 24.4 %collective-permute-start.13 = (bf16[224,1216]{1,0:T(8,128)(2,1)}, bf16[224,1216]{1,0:T(8,128)(2,1)S(1)}, u32[]{:S(2)}, u32[]{:S(2)}) collective-permute-start(bf16[224,1216]{1,0:T(8,128)(2,1)} %collective-permute-done.6.refs_10_), channel_id=1, source_target_pairs={{0,8},{8,16},{16,24},{24,28},{28,20},{20,12},{12,4},{4,0},{1,9},{9... | collective-permute-start | bytes 1634312 | tf_op jit(solution)/shard_map/ppermute | solution.py:211
  147.0 24.5 %collective-permute-start.14 = (bf16[224,1216]{1,0:T(8,128)(2,1)S(1)}, bf16[224,1216]{1,0:T(8,128)(2,1)S(1)}, u32[]{:S(2)}, u32[]{:S(2)}) collective-permute-start(bf16[224,1216]{1,0:T(8,128)(2,1)S(1)} %collective-permute-done.7.refs_13_), channel_id=1, source_target_pairs={{8,0},{16,8},{24,16},{28,24},{20,28},{12,20},{4,12},{0,4},{9,1},{1... | collective-permute-start | bytes 1634312 | tf_op jit(solution)/shard_map/ppermute | solution.py:215
  171.5 15.5 %collective-permute-start.16 = (bf16[192,1792]{1,0:T(8,128)(2,1)S(1)}, bf16[192,1792]{1,0:T(8,128)(2,1)S(1)}, u32[]{:S(2)}, u32[]{:S(2)}) collective-permute-start(bf16[192,1792]{1,0:T(8,128)(2,1)S(1)} %shard_map.146.refs_0_), channel_id=1, source_target_pairs={{0,2},{2,0},{1,3},{3,1},{4,6},{6,4},{5,7},{7,5},{8,10},{10,8},{9,1... | collective-permute-start | bytes 2064392 | tf_op jit(solution)/shard_map/ppermute | solution.py:362
  173.0 14.0 %collective-permute-start.18 = (bf16[224,1216]{1,0:T(8,128)(2,1)S(1)}, bf16[224,1216]{1,0:T(8,128)(2,1)S(1)}, u32[]{:S(2)}, u32[]{:S(2)}) collective-permute-start(bf16[224,1216]{1,0:T(8,128)(2,1)S(1)} %collective-permute-done.11.refs_3_), channel_id=1, source_target_pairs={{0,8},{8,16},{16,24},{24,28},{28,20},{20,12},{12,4},{4,0},{1,9},{9... | collective-permute-start | bytes 1634312 | tf_op jit(solution)/shard_map/ppermute | solution.py:211
  174.4 13.4 %collective-permute-start.19 = (bf16[224,1216]{1,0:T(8,128)(2,1)S(1)}, bf16[224,1216]{1,0:T(8,128)(2,1)S(1)}, u32[]{:S(2)}, u32[]{:S(2)}) collective-permute-start(bf16[224,1216]{1,0:T(8,128)(2,1)S(1)} %collective-permute-done.14.refs_14_), channel_id=1, source_target_pairs={{8,0},{16,8},{24,16},{28,24},{20,28},{12,20},{4,12},{0,4},{9,1},{1... | collective-permute-start | bytes 1634312 | tf_op jit(solution)/shard_map/ppermute | solution.py:215
  175.0 14.9 %collective-permute-start.15 = (bf16[192,1792]{1,0:T(8,128)(2,1)S(1)}, bf16[192,1792]{1,0:T(8,128)(2,1)S(1)}, u32[]{:S(2)}, u32[]{:S(2)}) collective-permute-start(bf16[192,1792]{1,0:T(8,128)(2,1)S(1)} %shard_map.146.refs_0_), channel_id=1, source_target_pairs={{0,1},{1,0},{2,3},{3,2},{4,5},{5,4},{6,7},{7,6},{8,9},{9,8},{10,11... | collective-permute-start | bytes 2064392 | tf_op jit(solution)/shard_map/ppermute | solution.py:358
  187.8 15.4 %collective-permute-start.20 = (bf16[224,1216]{1,0:T(8,128)(2,1)S(1)}, bf16[224,1216]{1,0:T(8,128)(2,1)S(1)}, u32[]{:S(2)}, u32[]{:S(2)}) collective-permute-start(bf16[224,1216]{1,0:T(8,128)(2,1)S(1)} %get-tuple-element.73.refs_0_), channel_id=1, source_target_pairs={{0,8},{8,16},{16,24},{24,28},{28,20},{20,12},{12,4},{4,0},{1,9},{9... | collective-permute-start | bytes 1634312 | tf_op jit(solution)/shard_map/ppermute | solution.py:211
  188.9 15.2 %collective-permute-start.21 = (bf16[224,1216]{1,0:T(8,128)(2,1)S(1)}, bf16[224,1216]{1,0:T(8,128)(2,1)}, u32[]{:S(2)}, u32[]{:S(2)}) collective-permute-start(bf16[224,1216]{1,0:T(8,128)(2,1)S(1)} %get-tuple-element.73.refs_0_), channel_id=1, source_target_pairs={{8,0},{16,8},{24,16},{28,24},{20,28},{12,20},{4,12},{0,4},{9,1},{1... | collective-permute-start | bytes 1634312 | tf_op jit(solution)/shard_map/ppermute | solution.py:215
  204.1 18.6 %collective-permute-start.22 = (bf16[224,1216]{1,0:T(8,128)(2,1)S(1)}, bf16[224,1216]{1,0:T(8,128)(2,1)}, u32[]{:S(2)}, u32[]{:S(2)}) collective-permute-start(bf16[224,1216]{1,0:T(8,128)(2,1)S(1)} %collective-permute-done.20.refs_1_), channel_id=1, source_target_pairs={{0,8},{8,16},{16,24},{24,28},{28,20},{20,12},{12,4},{4,0},{1,9},{9... | collective-permute-start | bytes 1634312 | tf_op jit(solution)/shard_map/ppermute | solution.py:211
  204.8 18.0 %collective-permute-start.23 = (bf16[224,1216]{1,0:T(8,128)(2,1)}, bf16[224,1216]{1,0:T(8,128)(2,1)}, u32[]{:S(2)}, u32[]{:S(2)}) collective-permute-start(bf16[224,1216]{1,0:T(8,128)(2,1)} %collective-permute-done.21.refs_3_), channel_id=1, source_target_pairs={{8,0},{16,8},{24,16},{28,24},{20,28},{12,20},{4,12},{0,4},{9,1},{1... | collective-permute-start | bytes 1634312 | tf_op jit(solution)/shard_map/ppermute | solution.py:215
  222.8 14.0 %collective-permute-start.24 = (bf16[224,1216]{1,0:T(8,128)(2,1)}, bf16[224,1216]{1,0:T(8,128)(2,1)S(1)}, u32[]{:S(2)}, u32[]{:S(2)}) collective-permute-start(bf16[224,1216]{1,0:T(8,128)(2,1)} %collective-permute-done.22.refs_2_), channel_id=1, source_target_pairs={{0,8},{8,16},{16,24},{24,28},{28,20},{20,12},{12,4},{4,0},{1,9},{9... | collective-permute-start | bytes 1634312 | tf_op jit(solution)/shard_map/ppermute | solution.py:211
  223.5 14.0 %collective-permute-start.25 = (bf16[224,1216]{1,0:T(8,128)(2,1)}, bf16[224,1216]{1,0:T(8,128)(2,1)S(1)}, u32[]{:S(2)}, u32[]{:S(2)}) collective-permute-start(bf16[224,1216]{1,0:T(8,128)(2,1)} %collective-permute-done.23.refs_4_), channel_id=1, source_target_pairs={{8,0},{16,8},{24,16},{28,24},{20,28},{12,20},{4,12},{0,4},{9,1},{1... | collective-permute-start | bytes 1634312 | tf_op jit(solution)/shard_map/ppermute | solution.py:215
  229.7 9.3 %collective-permute-start.29 = (bf16[192,1120]{1,0:T(8,128)(2,1)S(1)}, bf16[192,1120]{1,0:T(8,128)(2,1)S(1)}, u32[]{:S(2)}, u32[]{:S(2)}) collective-permute-start(bf16[192,1120]{1,0:T(8,128)(2,1)S(1)} %get-tuple-element.89), channel_id=1, source_target_pairs={{0,1},{1,0},{2,3},{3,2},{4,5},{5,4},{6,7},{7,6},{8,9},{9,8},{10,11... | collective-permute-start | bytes 1290248 | tf_op jit(solution)/shard_map/ppermute | solution.py:358
  229.7 17.4 %collective-permute-start.28 = (bf16[192,1120]{1,0:T(8,128)(2,1)S(1)}, bf16[192,1120]{1,0:T(8,128)(2,1)S(1)}, u32[]{:S(2)}, u32[]{:S(2)}) collective-permute-start(bf16[192,1120]{1,0:T(8,128)(2,1)S(1)} %get-tuple-element.87), channel_id=1, source_target_pairs={{0,1},{1,0},{2,3},{3,2},{4,5},{5,4},{6,7},{7,6},{8,9},{9,8},{10,11... | collective-permute-start | bytes 1290248 | tf_op jit(solution)/shard_map/ppermute | solution.py:358
  236.8 6.7 %collective-permute-start.26 = (bf16[112,1216]{1,0:T(8,128)(2,1)S(1)}, bf16[112,1216]{1,0:T(8,128)(2,1)S(1)}, u32[]{:S(2)}, u32[]{:S(2)}) collective-permute-start(bf16[112,1216]{1,0:T(8,128)(2,1)S(1)} %slice.40), channel_id=1, source_target_pairs={{0,8},{8,16},{16,24},{24,28},{28,20},{20,12},{12,4},{4,0},{1,9},{9... | collective-permute-start | bytes 817160 | tf_op jit(solution)/shard_map/ppermute | solution.py:211
  237.5 6.7 %collective-permute-start.27 = (bf16[112,1216]{1,0:T(8,128)(2,1)S(1)}, bf16[112,1216]{1,0:T(8,128)(2,1)S(1)}, u32[]{:S(2)}, u32[]{:S(2)}) collective-permute-start(bf16[112,1216]{1,0:T(8,128)(2,1)S(1)} %slice.41), channel_id=1, source_target_pairs={{8,0},{16,8},{24,16},{28,24},{20,28},{12,20},{4,12},{0,4},{9,1},{1... | collective-permute-start | bytes 817160 | tf_op jit(solution)/shard_map/ppermute | solution.py:215
  239.1 9.5 %collective-permute-start.30 = (bf16[192,1120]{1,0:T(8,128)(2,1)S(1)}, bf16[192,1120]{1,0:T(8,128)(2,1)S(1)}, u32[]{:S(2)}, u32[]{:S(2)}) collective-permute-start(bf16[192,1120]{1,0:T(8,128)(2,1)S(1)} %add_convert_fusion.2), channel_id=1, source_target_pairs={{0,2},{2,0},{1,3},{3,1},{4,6},{6,4},{5,7},{7,5},{8,10},{10,8},{9,1... | collective-permute-start | bytes 1290248 | tf_op jit(solution)/shard_map/ppermute | solution.py:362
  249.5 9.3 %collective-permute-start.33 = (bf16[192,672]{1,0:T(8,128)(2,1)}, bf16[192,672]{1,0:T(8,128)(2,1)}, u32[]{:S(2)}, u32[]{:S(2)}) collective-permute-start(bf16[192,672]{1,0:T(8,128)(2,1)} %add_convert_fusion.3), channel_id=1, source_target_pairs={{0,2},{2,0},{1,3},{3,1},{4,6},{6,4},{5,7},{7,5},{8,10},{10,8},{9,1... | collective-permute-start | bytes 774152 | tf_op jit(solution)/shard_map/ppermute | solution.py:362
  (35 other events, 601.0 us)
where the time goes:
time: 263 us; the launch traced here: 262 us
  waiting for transfers between devices  95.5 us (36%)
  Pallas kernels  57.2 us (22%)
  blocking collectives  40.9 us (16%)
  starting transfers between devices  36.2 us (14%)
  matrix products  16.7 us (6%)
  local copies, waits for them, and re-layouts  12.1 us (5%)
  other arithmetic  2.95 us (1%)
    psum x1, blocking collectives, per_device(): rank_feat = lax.psum(rank_part.astype(jnp.bfloat16), 'mdl')  40.9 us
    ppermute x11, waiting for transfers between devices, step_forward(): self.forward.append(lax.ppermute(self.forward[-1][rows], 'req', self.pairs))  39.2 us
    ppermute x11, waiting for transfers between devices, step_backward(): self.backward.append(lax.ppermute(self.backward[-1][rows], 'req', pairs))  35.2 us
    ppermute x4, waiting for transfers between devices, chip_swap(): return lax.ppermute(array, 'mdl', [(0, 2), (2, 0), (1, 3), (3, 1)])  21.1 us
    ppermute x11, starting transfers between devices, step_forward(): self.forward.append(lax.ppermute(self.forward[-1][rows], 'req', self.pairs))  18.3 us
    pallas_call x1, Pallas kernels, attention(): pl.pallas_call(attention_kernel, grid=(tokens // BLOCK,), in_specs=[own,...  15.7 us
    pallas_call x1, Pallas kernels, hidden_units(): pl.pallas_call(functools.partial(hidden_kernel, count), in_specs=[smem] +...  12.2 us
    pallas_call x1, Pallas kernels, project_and_normalise(): pl.pallas_call(project_kernel, in_specs=[smem] + [vmem] * 10, out_specs=[...  11.7 us
  transfers between devices with their start and end apart: 35, of which 17 were waited for; matrix products, arithmetic and copies ran while one was open for 8% of the time, Pallas kernels for 21%

commit v1 on v0

--- a/solution.py
+++ b/solution.py
@@ -13,7 +13,7 @@
 BLOCK = 192
 HALO = 64
 LANES = 256
-VMEM_LIMIT = 48 * 1024 * 1024
+VMEM_LIMIT = 28 * 1024 * 1024
 NT = (((1,), (1,)), ((), ()))
 SMALL = pl.CostEstimate(flops=0, bytes_accessed=0, transcendentals=0)
 
@@ -436,7 +436,7 @@
         down_origins = ring_origins(req_index, req_devices, near_steps + far_steps)
         gate, up = Ring(feedforward_weight[0], req_devices), Ring(feedforward_weight[1], req_devices)
         step(gate, up)
-        (packed,) = tie([gate, up], packed)
+        (packed,) = tie([gate], packed)
         step(gate, up)
     arrived = lax.all_to_all(packed, "req", split_axis=0, concat_axis=0, tiled=True)
 

time: 263 us -> 268 us (1.019)
  starting transfers between devices: 36.2 us -> 57.2 us
  waiting for transfers between devices: 95.5 us -> 75.8 us
  local copies, waits for them, and re-layouts: 12.1 us -> 24.8 us
  Pallas kernels: 57.2 us -> 47.8 us
    ppermute x11, starting transfers between devices: 18.3 us -> 38.5 us  [step_forward(): self.forward.append(lax.ppermute(self.forward[-1][rows], 'req', self.pairs))]
    ppermute x11, waiting for transfers between devices: 35.2 us -> 20.7 us  [step_backward(): self.backward.append(lax.ppermute(self.backward[-1][rows], 'req', pairs))]
    unnamed x65 -> x71, local copies, waits for them, and re-layouts: 9.43 us -> 22.1 us
    ppermute x11, waiting for transfers between devices: 39.2 us -> 34.7 us  [step_forward(): self.forward.append(lax.ppermute(self.forward[-1][rows], 'req', self.pairs))]
    pallas_call x1, Pallas kernels: 7.07 us -> 3.11 us  [pack_windows(): pl.pallas_call(functools.partial(pack_kernel, cap), grid_spec=pltpu.Prefe...]
  transfers between devices with their start and end apart: 35 -> 35, of which waited for: 17 -> 17; matrix products, arithmetic and copies ran while one was open for 8% -> 8% of each run, Pallas kernels for 21% -> 17%
where the time goes in v1:
time: 268 us; the launch traced here: 267 us
  waiting for transfers between devices  75.8 us (28%)
  starting transfers between devices  57.2 us (21%)
  Pallas kernels  47.8 us (18%)
  blocking collectives  40.9 us (15%)
  local copies, waits for them, and re-layouts  24.8 us (9%)
  matrix products  16.7 us (6%)
  other arithmetic  3.05 us (1%)
    psum x1, blocking collectives, per_device(): rank_feat = lax.psum(rank_part.astype(jnp.bfloat16), 'mdl')  40.9 us
    ppermute x11, starting transfers between devices, step_forward(): self.forward.append(lax.ppermute(self.forward[-1][rows], 'req', self.pairs))  38.5 us
    ppermute x11, waiting for transfers between devices, step_forward(): self.forward.append(lax.ppermute(self.forward[-1][rows], 'req', self.pairs))  34.7 us
    unnamed x71, local copies, waits for them, and re-layouts  22.1 us
    ppermute x11, waiting for transfers between devices, step_backward(): self.backward.append(lax.ppermute(self.backward[-1][rows], 'req', pairs))  20.7 us
    ppermute x4, waiting for transfers between devices, chip_swap(): return lax.ppermute(array, 'mdl', [(0, 2), (2, 0), (1, 3), (3, 1)])  19.2 us
    pallas_call x1, Pallas kernels, attention(): pl.pallas_call(attention_kernel, grid=(tokens // BLOCK,), in_specs=[own,...  15.8 us
    dot_general x3, matrix products, per_device(): lax.dot_general(stream, attention_projection_weight[k], NT, preferred_ele...  10.9 us
  transfers between devices with their start and end apart: 35, of which 17 were waited for; matrix products, arithmetic and copies ran while one was open for 8% of the time, Pallas kernels for 17%

profile of v1, /device:TPU:0, one launch (start us, length us, event | category | flops | bytes accessed | tf_op | source)
XLA Modules:
  0.0 266.8 jit_solution(12644828993530663715)
XLA Ops:
  1.6 3.1 %collective-permute-start = (bf16[224,1216]{1,0:T(8,128)(2,1)S(1)}, bf16[224,1216]{1,0:T(8,128)(2,1)S(1)}, u32[]{:S(2)}, u32[]{:S(2)}) collective-permute-start(bf16[224,1216]{1,0:T(8,128)(2,1)S(1)} %get-tuple-element.96.refs_0_), channel_id=1, source_target_pairs={{0,8},{8,16},{16,24},{24,28},{28,20},{20,12},{12,4},{4,0},{1,9},{9... | collective-permute-start | bytes 1634312 | tf_op jit(solution)/shard_map/ppermute | solution.py:211
  6.9 3.1 %copy-done.2 = bf16[32,2,448,128]{3,2,1,0:T(8,128)(2,1)S(1)} copy-done((bf16[32,2,448,128]{3,2,1,0:T(8,128)(2,1)S(1)}, bf16[32,2,448,128]{3,2,1,0:T(8,128)(2,1)}, u32[]{:S(2)}) %copy-start.2) | copy-done | bytes 7340056
  10.0 3.1 %shard_map.145 = bf16[8,2,2,448,128]{4,3,2,1,0:T(8,128)(2,1)S(1)} custom-call(s32[32]{0:T(128)S(1)} %reshape.124.table_ref, s32[32]{0:T(128)S(1)} %reshape.125.offset_ref, bf16[32,2,448,128]{3,2,1,0:T(8,128)(2,1)S(1)} %copy-done.2, bf16[32,2,448,128]{3,2,1,0:T(8,128)(2,1)S(1)} %copy-done.2, bf16[32,2,448,128]{3,2,1,0:T(8,128)(2,1)S(1)} %copy-done.2, ...), custom_call_target="tpu_custom_call" | custom-call | tf_op jit(solution)/shard_map/pallas_call | solution.py:45
  14.9 2.7 %collective-permute-done.refs_1_ = bf16[224,1216]{1,0:T(8,128)(2,1)S(1)} collective-permute-done((bf16[224,1216]{1,0:T(8,128)(2,1)S(1)}, bf16[224,1216]{1,0:T(8,128)(2,1)S(1)}, u32[]{:S(2)}, u32[]{:S(2)}) %collective-permute-start) | collective-permute-done | bytes 544800 | tf_op jit(solution)/shard_map/ppermute | solution.py:211
  19.2 4.8 %all-to-all-start = ((bf16[8,2,2,448,128]{4,3,2,1,0:T(8,128)(2,1)}), bf16[8,2,2,448,128]{4,3,2,1,0:T(8,128)(2,1)}, u32[]{:S(2)}, u32[]{:S(2)}) async-start(bf16[8,2,2,448,128]{4,3,2,1,0:T(8,128)(2,1)} %copy-done.3), calls=%async_computation | async-start | bytes 7340032 | tf_op jit(solution)/shard_map/all_to_all | solution.py:441
  24.1 2.0 collective-permute-start.4
  27.7 2.7 %fusion.24 = f32[768,256]{0,1:S(1)} fusion(bf16[768,1792]{1,0:T(8,128)(2,1)} %refs_8_.1, bf16[1792,256]{0,1:T(8,128)(2,1)S(1)} %bitcast.62), kind=kOutput, calls=%fused_computation.55 | convolution fusion | flops 704643072 | bytes 4456448
  30.5 40.9 %psum.7 = bf16[768,16]{0,1:T(8,128)(2,1)S(1)} all-reduce(bf16[768,16]{0,1:T(8,128)(2,1)S(1)} %multiply_reduce_fusion), channel_id=1, replica_groups=mesh['req'=8,'mdl'=4] {'mdl'}, use_global_device_ids=true, to_apply=%region_7.8 | all-reduce | flops 12288 | bytes 49152 | tf_op jit(solution)/shard_map/psum | solution.py:458
  71.9 4.0 %fusion.4 = f32[768,448]{1,0:T(8,128)S(1)} fusion(bf16[768,1792]{1,0:T(8,128)(2,1)} %refs_8_.1, bf16[3,448,1792]{2,1,0:T(8,128)(2,1)} %param.16), kind=kOutput, calls=%fused_computation.4 | convolution fusion | flops 1233125376 | bytes 5734400 | tf_op jit(solution)/shard_map/dot_general | solution.py:444
  75.9 2.0 collective-permute-start.2
  78.0 2.1 add_convert_fusion.1.query_ref
  80.1 3.0 %fusion = f32[768,448]{1,0:T(8,128)S(1)} fusion(bf16[768,1792]{1,0:T(8,128)(2,1)S(1)} %copy-done.4, bf16[3,448,1792]{2,1,0:T(8,128)(2,1)} %param.16), kind=kOutput, calls=%fused_computation | convolution fusion | flops 1233125376 | bytes 5734400 | tf_op jit(solution)/shard_map/dot_general | solution.py:444
  83.1 14.3 %collective-permute-done.4.refs_9_ = bf16[224,1216]{1,0:T(8,128)(2,1)} collective-permute-done((bf16[224,1216]{1,0:T(8,128)(2,1)S(1)}, bf16[224,1216]{1,0:T(8,128)(2,1)}, u32[]{:S(2)}, u32[]{:S(2)}) %collective-permute-start.4) | collective-permute-done | bytes 544800 | tf_op jit(solution)/shard_map/ppermute | solution.py:211
  97.4 20.4 %collective-permute-start.5 = (bf16[224,1216]{1,0:T(8,128)(2,1)}, bf16[224,1216]{1,0:T(8,128)(2,1)}, u32[]{:S(2)}, u32[]{:S(2)}) collective-permute-start(bf16[224,1216]{1,0:T(8,128)(2,1)} %collective-permute-done.4.refs_9_), channel_id=1, source_target_pairs={{0,8},{8,16},{16,24},{24,28},{28,20},{20,12},{12,4},{4,0},{1,9},{9... | collective-permute-start | bytes 1634312 | tf_op jit(solution)/shard_map/ppermute | solution.py:211
  117.8 2.6 collective-permute-start.7
  121.6 3.8 %fusion.9.key_before_ref.key_ref = bf16[768,448]{1,0:T(8,128)(2,1)S(1)} fusion(bf16[768,1792]{1,0:T(8,128)(2,1)} %refs_8_.1, bf16[3,448,1792]{2,1,0:T(8,128)(2,1)} %param.16), kind=kOutput, calls=%fused_computation.11 | convolution fusion | flops 1233469440 | bytes 5046272 | tf_op jit(solution)/shard_map/dot_general | solution.py:444
  125.4 4.7 %collective-permute-done.3.refs_6_ = bf16[224,1216]{1,0:T(8,128)(2,1)} collective-permute-done((bf16[224,1216]{1,0:T(8,128)(2,1)}, bf16[224,1216]{1,0:T(8,128)(2,1)}, u32[]{:S(2)}, u32[]{:S(2)}) %collective-permute-start.3) | collective-permute-done | bytes 544800 | tf_op jit(solution)/shard_map/ppermute | solution.py:215
  131.5 10.9 %collective-permute-done.7.refs_13_ = bf16[224,1216]{1,0:T(8,128)(2,1)} collective-permute-done((bf16[224,1216]{1,0:T(8,128)(2,1)}, bf16[224,1216]{1,0:T(8,128)(2,1)}, u32[]{:S(2)}, u32[]{:S(2)}) %collective-permute-start.7) | collective-permute-done | bytes 544800 | tf_op jit(solution)/shard_map/ppermute | solution.py:215
  142.4 2.6 collective-permute-start.11
  145.1 2.0 collective-permute-start.13
  148.9 15.8 %shard_map.146.refs_0_ = bf16[192,1792]{1,0:T(8,128)(2,1)S(1)} custom-call(bf16[768,448]{1,0:T(8,128)(2,1)S(1)} %copy-done.9, bf16[768,448]{1,0:T(8,128)(2,1)S(1)} %fusion.9.key_before_ref.key_ref, bf16[768,448]{1,0:T(8,128)(2,1)S(1)} %fusion.9.key_before_ref.key_ref, bf16[768,448]{1,0:T(8,128)(2,1)S(1)} %add_convert_fusion.value_before_ref.value_ref, ...), custom_call_target="tpu_custom_call" | custom-call | tf_op jit(solution)/shard_map/pallas_call | solution.py:125
  165.5 3.9 %collective-permute-done.13.refs_11_ = bf16[224,1216]{1,0:T(8,128)(2,1)S(1)} collective-permute-done((bf16[224,1216]{1,0:T(8,128)(2,1)}, bf16[224,1216]{1,0:T(8,128)(2,1)S(1)}, u32[]{:S(2)}, u32[]{:S(2)}) %collective-permute-start.13) | collective-permute-done | bytes 544800 | tf_op jit(solution)/shard_map/ppermute | solution.py:211
  175.9 11.2 %collective-permute-done.16.refs_2_ = bf16[192,1792]{1,0:T(8,128)(2,1)S(1)} collective-permute-done((bf16[192,1792]{1,0:T(8,128)(2,1)S(1)}, bf16[192,1792]{1,0:T(8,128)(2,1)S(1)}, u32[]{:S(2)}, u32[]{:S(2)}) %collective-permute-start.16) | collective-permute-done | bytes 688160 | tf_op jit(solution)/shard_map/ppermute | solution.py:362
  190.8 9.3 %shard_map.147 = (bf16[768,1792]{1,0:T(8,128)(2,1)S(1)}, bf16[192,1792]{1,0:T(8,128)(2,1)S(1)}) custom-call(s32[1]{0:T(128)} %bitcast.8.place_ref, bf16[192,1792]{1,0:T(8,128)(2,1)S(1)} %shard_map.146.refs_0_, bf16[192,1792]{1,0:T(8,128)(2,1)S(1)} %collective-permute-done.15.refs_1_, bf16[192,1792]{1,0:T(8,128)(2,1)S(1)} %collective-permute-done.16.refs_2_, ...), custom_call_target="tpu_custom_call" | custom-call | tf_op jit(solution)/shard_map/pallas_call | solution.py:178
  201.6 2.6 collective-permute-done.20.refs_1_
  216.6 9.6 %shard_map.148.hidden_ref = bf16[768,1216]{1,0:T(8,128)(2,1)S(1)} custom-call(s32[16]{0:T(128)S(1)} %stack.58.origin_ref, bf16[224,1216]{1,0:T(8,128)(2,1)S(1)} %get-tuple-element.96.refs_0_, bf16[224,1216]{1,0:T(8,128)(2,1)S(1)} %copy-done.11, bf16[224,1216]{1,0:T(8,128)(2,1)} %collective-permute-done.2.refs_2_, bf16[224,1216]{1,0:T(8,128)(2,1)S(1)} %copy-done.13, ...), custom_call_target="tpu_custom_call" | custom-call | tf_op jit(solution)/shard_map/pallas_call | solution.py:275
  228.3 4.4 %shard_map.150 = (bf16[192,1120]{1,0:T(8,128)(2,1)S(1)}, bf16[192,1120]{1,0:T(8,128)(2,1)S(1)}, bf16[192,1120]{1,0:T(8,128)(2,1)S(1)}, bf16[192,1120]{1,0:T(8,128)(2,1)S(1)}) custom-call(bf16[768,1216]{1,0:T(8,128)(2,1)S(1)} %shard_map.148.hidden_ref, bf16[224,1216]{1,0:T(8,128)(2,1)S(1)} %get-tuple-element.69.refs_0_, ...), custom_call_target="tpu_custom_call" | custom-call | tf_op jit(solution)/shard_map/pallas_call | solution.py:311
  233.3 7.0 %collective-permute-done.24.refs_0_ = bf16[224,1216]{1,0:T(8,128)(2,1)S(1)} collective-permute-done((bf16[224,1216]{1,0:T(8,128)(2,1)}, bf16[224,1216]{1,0:T(8,128)(2,1)S(1)}, u32[]{:S(2)}, u32[]{:S(2)}) %collective-permute-start.24) | collective-permute-done | bytes 544800 | tf_op jit(solution)/shard_map/ppermute | solution.py:211
  244.1 2.9 %collective-permute-done.26.refs_2_ = bf16[112,1216]{1,0:T(8,128)(2,1)S(1)} collective-permute-done((bf16[112,1216]{1,0:T(8,128)(2,1)S(1)}, bf16[112,1216]{1,0:T(8,128)(2,1)S(1)}, u32[]{:S(2)}, u32[]{:S(2)}) %collective-permute-start.26) | collective-permute-done | bytes 272416 | tf_op jit(solution)/shard_map/ppermute | solution.py:211
  248.1 2.4 shard_map.149
  255.7 7.8 %collective-permute-done.33.refs_3_ = bf16[192,672]{1,0:T(8,128)(2,1)} collective-permute-done((bf16[192,672]{1,0:T(8,128)(2,1)}, bf16[192,672]{1,0:T(8,128)(2,1)}, u32[]{:S(2)}, u32[]{:S(2)}) %collective-permute-start.33) | collective-permute-done | bytes 258080 | tf_op jit(solution)/shard_map/ppermute | solution.py:362
  263.5 3.3 %shard_map.151 = bf16[192,1792]{1,0:T(8,128)(2,1)} custom-call(s32[8]{0:T(128)S(1)} %stack.56.origin_ref, bf16[192,1792]{1,0:T(8,128)(2,1)S(1)} %get-tuple-element.64.resid_ref, f32[192,1120]{1,0:T(8,128)S(1)} %convert_add_fusion.refs_0_, bf16[192,672]{1,0:T(8,128)(2,1)S(1)} %copy-done.25, bf16[192,672]{1,0:T(8,128)(2,1)S(1)} %collective-permute-done.31.refs_2_, ...), custom_call_target="tpu_custom_call" | custom-call | tf_op jit(solution)/shard_map/pallas_call | solution.py:346
  (160 shorter events, 51.3 us)
Async XLA Ops:
  1.6 16.0 %collective-permute-start = (bf16[224,1216]{1,0:T(8,128)(2,1)S(1)}, bf16[224,1216]{1,0:T(8,128)(2,1)S(1)}, u32[]{:S(2)}, u32[]{:S(2)}) collective-permute-start(bf16[224,1216]{1,0:T(8,128)(2,1)S(1)} %get-tuple-element.96.refs_0_), channel_id=1, source_target_pairs={{0,8},{8,16},{16,24},{24,28},{28,20},{20,12},{12,4},{4,0},{1,9},{9... | collective-permute-start | bytes 1634312 | tf_op jit(solution)/shard_map/ppermute | solution.py:211
  4.7 14.5 %collective-permute-start.1 = (bf16[224,1216]{1,0:T(8,128)(2,1)S(1)}, bf16[224,1216]{1,0:T(8,128)(2,1)}, u32[]{:S(2)}, u32[]{:S(2)}) collective-permute-start(bf16[224,1216]{1,0:T(8,128)(2,1)S(1)} %get-tuple-element.96.refs_0_), channel_id=1, source_target_pairs={{8,0},{16,8},{24,16},{28,24},{20,28},{12,20},{4,12},{0,4},{9,1},{1... | collective-permute-start | bytes 1634312 | tf_op jit(solution)/shard_map/ppermute | solution.py:215
  19.2 123.2 %all-to-all-start = ((bf16[8,2,2,448,128]{4,3,2,1,0:T(8,128)(2,1)}), bf16[8,2,2,448,128]{4,3,2,1,0:T(8,128)(2,1)}, u32[]{:S(2)}, u32[]{:S(2)}) async-start(bf16[8,2,2,448,128]{4,3,2,1,0:T(8,128)(2,1)} %copy-done.3), calls=%async_computation | async-start | bytes 7340032 | tf_op jit(solution)/shard_map/all_to_all | solution.py:441
  24.1 73.3 %collective-permute-start.4 = (bf16[224,1216]{1,0:T(8,128)(2,1)S(1)}, bf16[224,1216]{1,0:T(8,128)(2,1)}, u32[]{:S(2)}, u32[]{:S(2)}) collective-permute-start(bf16[224,1216]{1,0:T(8,128)(2,1)S(1)} %get-tuple-element.97.refs_8_), channel_id=1, source_target_pairs={{0,8},{8,16},{16,24},{24,28},{28,20},{20,12},{12,4},{4,0},{1,9},{9... | collective-permute-start | bytes 1634312 | tf_op jit(solution)/shard_map/ppermute | solution.py:211
  26.1 71.3 %collective-permute-start.6 = (bf16[224,1216]{1,0:T(8,128)(2,1)S(1)}, bf16[224,1216]{1,0:T(8,128)(2,1)}, u32[]{:S(2)}, u32[]{:S(2)}) collective-permute-start(bf16[224,1216]{1,0:T(8,128)(2,1)S(1)} %get-tuple-element.97.refs_8_), channel_id=1, source_target_pairs={{8,0},{16,8},{24,16},{28,24},{20,28},{12,20},{4,12},{0,4},{9,1},{1... | collective-permute-start | bytes 1634312 | tf_op jit(solution)/shard_map/ppermute | solution.py:215
  26.1 116.3 %collective-permute-start.8 = (bf16[448,1792]{1,0:T(8,128)(2,1)}, bf16[448,1792]{1,0:T(8,128)(2,1)}, u32[]{:S(2)}, u32[]{:S(2)}) collective-permute-start(bf16[448,1792]{1,0:T(8,128)(2,1)} %refs_4_), channel_id=1, source_target_pairs={{0,1},{1,0},{2,3},{3,2},{4,5},{5,4},{6,7},{7,6},{8,9},{9,8},{10,11... | collective-permute-start | bytes 4816904 | tf_op jit(solution)/shard_map/ppermute | solution.py:358
  26.1 51.9 %collective-permute-start.9 = (bf16[448,1792]{1,0:T(8,128)(2,1)}, bf16[448,1792]{1,0:T(8,128)(2,1)}, u32[]{:S(2)}, u32[]{:S(2)}) collective-permute-start(bf16[448,1792]{1,0:T(8,128)(2,1)} %refs_4_), channel_id=1, source_target_pairs={{0,2},{2,0},{1,3},{3,1},{4,6},{6,4},{5,7},{7,5},{8,10},{10,8},{9,1... | collective-permute-start | bytes 4816904 | tf_op jit(solution)/shard_map/ppermute | solution.py:362
  75.9 41.9 %collective-permute-start.2 = (bf16[224,1216]{1,0:T(8,128)(2,1)S(1)}, bf16[224,1216]{1,0:T(8,128)(2,1)}, u32[]{:S(2)}, u32[]{:S(2)}) collective-permute-start(bf16[224,1216]{1,0:T(8,128)(2,1)S(1)} %collective-permute-done.refs_1_), channel_id=1, source_target_pairs={{0,8},{8,16},{16,24},{24,28},{28,20},{20,12},{12,4},{4,0},{1,9},{9... | collective-permute-start | bytes 1634312 | tf_op jit(solution)/shard_map/ppermute | solution.py:211
  78.0 64.4 %collective-permute-start.10 = (bf16[448,1792]{1,0:T(8,128)(2,1)}, bf16[448,1792]{1,0:T(8,128)(2,1)}, u32[]{:S(2)}, u32[]{:S(2)}) collective-permute-start(bf16[448,1792]{1,0:T(8,128)(2,1)} %collective-permute-done.9.refs_6_), channel_id=1, source_target_pairs={{0,1},{1,0},{2,3},{3,2},{4,5},{5,4},{6,7},{7,6},{8,9},{9,8},{10,11... | collective-permute-start | bytes 4816904 | tf_op jit(solution)/shard_map/ppermute | solution.py:358
  97.4 32.7 %collective-permute-start.3 = (bf16[224,1216]{1,0:T(8,128)(2,1)}, bf16[224,1216]{1,0:T(8,128)(2,1)}, u32[]{:S(2)}, u32[]{:S(2)}) collective-permute-start(bf16[224,1216]{1,0:T(8,128)(2,1)} %collective-permute-done.1.refs_5_), channel_id=1, source_target_pairs={{8,0},{16,8},{24,16},{28,24},{20,28},{12,20},{4,12},{0,4},{9,1},{1... | collective-permute-start | bytes 1634312 | tf_op jit(solution)/shard_map/ppermute | solution.py:215
  97.4 34.2 %collective-permute-start.5 = (bf16[224,1216]{1,0:T(8,128)(2,1)}, bf16[224,1216]{1,0:T(8,128)(2,1)}, u32[]{:S(2)}, u32[]{:S(2)}) collective-permute-start(bf16[224,1216]{1,0:T(8,128)(2,1)} %collective-permute-done.4.refs_9_), channel_id=1, source_target_pairs={{0,8},{8,16},{16,24},{24,28},{28,20},{20,12},{12,4},{4,0},{1,9},{9... | collective-permute-start | bytes 1634312 | tf_op jit(solution)/shard_map/ppermute | solution.py:211
  117.8 24.6 %collective-permute-start.7 = (bf16[224,1216]{1,0:T(8,128)(2,1)}, bf16[224,1216]{1,0:T(8,128)(2,1)}, u32[]{:S(2)}, u32[]{:S(2)}) collective-permute-start(bf16[224,1216]{1,0:T(8,128)(2,1)} %collective-permute-done.6.refs_12_), channel_id=1, source_target_pairs={{8,0},{16,8},{24,16},{28,24},{20,28},{12,20},{4,12},{0,4},{9,1},{1... | collective-permute-start | bytes 1634312 | tf_op jit(solution)/shard_map/ppermute | solution.py:215
  142.4 22.2 %collective-permute-start.11 = (bf16[224,1216]{1,0:T(8,128)(2,1)}, bf16[224,1216]{1,0:T(8,128)(2,1)S(1)}, u32[]{:S(2)}, u32[]{:S(2)}) collective-permute-start(bf16[224,1216]{1,0:T(8,128)(2,1)} %collective-permute-done.2.refs_2_), channel_id=1, source_target_pairs={{0,8},{8,16},{16,24},{24,28},{28,20},{20,12},{12,4},{4,0},{1,9},{9... | collective-permute-start | bytes 1634312 | tf_op jit(solution)/shard_map/ppermute | solution.py:211
  145.1 19.6 %collective-permute-start.12 = (bf16[224,1216]{1,0:T(8,128)(2,1)}, bf16[224,1216]{1,0:T(8,128)(2,1)S(1)}, u32[]{:S(2)}, u32[]{:S(2)}) collective-permute-start(bf16[224,1216]{1,0:T(8,128)(2,1)} %collective-permute-done.3.refs_6_), channel_id=1, source_target_pairs={{8,0},{16,8},{24,16},{28,24},{20,28},{12,20},{4,12},{0,4},{9,1},{1... | collective-permute-start | bytes 1634312 | tf_op jit(solution)/shard_map/ppermute | solution.py:215
  145.1 24.4 %collective-permute-start.13 = (bf16[224,1216]{1,0:T(8,128)(2,1)}, bf16[224,1216]{1,0:T(8,128)(2,1)S(1)}, u32[]{:S(2)}, u32[]{:S(2)}) collective-permute-start(bf16[224,1216]{1,0:T(8,128)(2,1)} %collective-permute-done.5.refs_10_), channel_id=1, source_target_pairs={{0,8},{8,16},{16,24},{24,28},{28,20},{20,12},{12,4},{4,0},{1,9},{9... | collective-permute-start | bytes 1634312 | tf_op jit(solution)/shard_map/ppermute | solution.py:211
  147.1 24.5 %collective-permute-start.14 = (bf16[224,1216]{1,0:T(8,128)(2,1)}, bf16[224,1216]{1,0:T(8,128)(2,1)S(1)}, u32[]{:S(2)}, u32[]{:S(2)}) collective-permute-start(bf16[224,1216]{1,0:T(8,128)(2,1)} %collective-permute-done.7.refs_13_), channel_id=1, source_target_pairs={{8,0},{16,8},{24,16},{28,24},{20,28},{12,20},{4,12},{0,4},{9,1},{1... | collective-permute-start | bytes 1634312 | tf_op jit(solution)/shard_map/ppermute | solution.py:215
  171.5 15.5 %collective-permute-start.16 = (bf16[192,1792]{1,0:T(8,128)(2,1)S(1)}, bf16[192,1792]{1,0:T(8,128)(2,1)S(1)}, u32[]{:S(2)}, u32[]{:S(2)}) collective-permute-start(bf16[192,1792]{1,0:T(8,128)(2,1)S(1)} %shard_map.146.refs_0_), channel_id=1, source_target_pairs={{0,2},{2,0},{1,3},{3,1},{4,6},{6,4},{5,7},{7,5},{8,10},{10,8},{9,1... | collective-permute-start | bytes 2064392 | tf_op jit(solution)/shard_map/ppermute | solution.py:362
  173.0 14.0 %collective-permute-start.18 = (bf16[224,1216]{1,0:T(8,128)(2,1)S(1)}, bf16[224,1216]{1,0:T(8,128)(2,1)S(1)}, u32[]{:S(2)}, u32[]{:S(2)}) collective-permute-start(bf16[224,1216]{1,0:T(8,128)(2,1)S(1)} %collective-permute-done.11.refs_3_), channel_id=1, source_target_pairs={{0,8},{8,16},{16,24},{24,28},{28,20},{20,12},{12,4},{4,0},{1,9},{9... | collective-permute-start | bytes 1634312 | tf_op jit(solution)/shard_map/ppermute | solution.py:211
  174.5 13.4 %collective-permute-start.19 = (bf16[224,1216]{1,0:T(8,128)(2,1)S(1)}, bf16[224,1216]{1,0:T(8,128)(2,1)S(1)}, u32[]{:S(2)}, u32[]{:S(2)}) collective-permute-start(bf16[224,1216]{1,0:T(8,128)(2,1)S(1)} %collective-permute-done.14.refs_14_), channel_id=1, source_target_pairs={{8,0},{16,8},{24,16},{28,24},{20,28},{12,20},{4,12},{0,4},{9,1},{1... | collective-permute-start | bytes 1634312 | tf_op jit(solution)/shard_map/ppermute | solution.py:215
  175.9 14.9 %collective-permute-start.15 = (bf16[192,1792]{1,0:T(8,128)(2,1)S(1)}, bf16[192,1792]{1,0:T(8,128)(2,1)S(1)}, u32[]{:S(2)}, u32[]{:S(2)}) collective-permute-start(bf16[192,1792]{1,0:T(8,128)(2,1)S(1)} %shard_map.146.refs_0_), channel_id=1, source_target_pairs={{0,1},{1,0},{2,3},{3,2},{4,5},{5,4},{6,7},{7,6},{8,9},{9,8},{10,11... | collective-permute-start | bytes 2064392 | tf_op jit(solution)/shard_map/ppermute | solution.py:358
  188.7 15.5 %collective-permute-start.20 = (bf16[224,1216]{1,0:T(8,128)(2,1)S(1)}, bf16[224,1216]{1,0:T(8,128)(2,1)}, u32[]{:S(2)}, u32[]{:S(2)}) collective-permute-start(bf16[224,1216]{1,0:T(8,128)(2,1)S(1)} %get-tuple-element.69.refs_0_), channel_id=1, source_target_pairs={{0,8},{8,16},{16,24},{24,28},{28,20},{20,12},{12,4},{4,0},{1,9},{9... | collective-permute-start | bytes 1634312 | tf_op jit(solution)/shard_map/ppermute | solution.py:211
  190.1 15.2 %collective-permute-start.21 = (bf16[224,1216]{1,0:T(8,128)(2,1)S(1)}, bf16[224,1216]{1,0:T(8,128)(2,1)}, u32[]{:S(2)}, u32[]{:S(2)}) collective-permute-start(bf16[224,1216]{1,0:T(8,128)(2,1)S(1)} %get-tuple-element.69.refs_0_), channel_id=1, source_target_pairs={{8,0},{16,8},{24,16},{28,24},{20,28},{12,20},{4,12},{0,4},{9,1},{1... | collective-permute-start | bytes 1634312 | tf_op jit(solution)/shard_map/ppermute | solution.py:215
  205.3 20.9 %collective-permute-start.22 = (bf16[224,1216]{1,0:T(8,128)(2,1)}, bf16[224,1216]{1,0:T(8,128)(2,1)}, u32[]{:S(2)}, u32[]{:S(2)}) collective-permute-start(bf16[224,1216]{1,0:T(8,128)(2,1)} %collective-permute-done.20.refs_1_), channel_id=1, source_target_pairs={{0,8},{8,16},{16,24},{24,28},{28,20},{20,12},{12,4},{4,0},{1,9},{9... | collective-permute-start | bytes 1634312 | tf_op jit(solution)/shard_map/ppermute | solution.py:211
  206.4 19.8 %collective-permute-start.23 = (bf16[224,1216]{1,0:T(8,128)(2,1)}, bf16[224,1216]{1,0:T(8,128)(2,1)}, u32[]{:S(2)}, u32[]{:S(2)}) collective-permute-start(bf16[224,1216]{1,0:T(8,128)(2,1)} %collective-permute-done.21.refs_3_), channel_id=1, source_target_pairs={{8,0},{16,8},{24,16},{28,24},{20,28},{12,20},{4,12},{0,4},{9,1},{1... | collective-permute-start | bytes 1634312 | tf_op jit(solution)/shard_map/ppermute | solution.py:215
  226.2 14.0 %collective-permute-start.24 = (bf16[224,1216]{1,0:T(8,128)(2,1)}, bf16[224,1216]{1,0:T(8,128)(2,1)S(1)}, u32[]{:S(2)}, u32[]{:S(2)}) collective-permute-start(bf16[224,1216]{1,0:T(8,128)(2,1)} %collective-permute-done.22.refs_2_), channel_id=1, source_target_pairs={{0,8},{8,16},{16,24},{24,28},{28,20},{20,12},{12,4},{4,0},{1,9},{9... | collective-permute-start | bytes 1634312 | tf_op jit(solution)/shard_map/ppermute | solution.py:211
  227.4 14.0 %collective-permute-start.25 = (bf16[224,1216]{1,0:T(8,128)(2,1)}, bf16[224,1216]{1,0:T(8,128)(2,1)S(1)}, u32[]{:S(2)}, u32[]{:S(2)}) collective-permute-start(bf16[224,1216]{1,0:T(8,128)(2,1)} %collective-permute-done.23.refs_4_), channel_id=1, source_target_pairs={{8,0},{16,8},{24,16},{28,24},{20,28},{12,20},{4,12},{0,4},{9,1},{1... | collective-permute-start | bytes 1634312 | tf_op jit(solution)/shard_map/ppermute | solution.py:215
  232.7 9.7 %collective-permute-start.29 = (bf16[192,1120]{1,0:T(8,128)(2,1)S(1)}, bf16[192,1120]{1,0:T(8,128)(2,1)S(1)}, u32[]{:S(2)}, u32[]{:S(2)}) collective-permute-start(bf16[192,1120]{1,0:T(8,128)(2,1)S(1)} %get-tuple-element.85), channel_id=1, source_target_pairs={{0,1},{1,0},{2,3},{3,2},{4,5},{5,4},{6,7},{7,6},{8,9},{9,8},{10,11... | collective-permute-start | bytes 1290248 | tf_op jit(solution)/shard_map/ppermute | solution.py:358
  232.8 19.0 %collective-permute-start.28 = (bf16[192,1120]{1,0:T(8,128)(2,1)S(1)}, bf16[192,1120]{1,0:T(8,128)(2,1)S(1)}, u32[]{:S(2)}, u32[]{:S(2)}) collective-permute-start(bf16[192,1120]{1,0:T(8,128)(2,1)S(1)} %get-tuple-element.83), channel_id=1, source_target_pairs={{0,1},{1,0},{2,3},{3,2},{4,5},{5,4},{6,7},{7,6},{8,9},{9,8},{10,11... | collective-permute-start | bytes 1290248 | tf_op jit(solution)/shard_map/ppermute | solution.py:358
  240.3 6.7 %collective-permute-start.26 = (bf16[112,1216]{1,0:T(8,128)(2,1)S(1)}, bf16[112,1216]{1,0:T(8,128)(2,1)S(1)}, u32[]{:S(2)}, u32[]{:S(2)}) collective-permute-start(bf16[112,1216]{1,0:T(8,128)(2,1)S(1)} %slice.40), channel_id=1, source_target_pairs={{0,8},{8,16},{16,24},{24,28},{28,20},{20,12},{12,4},{4,0},{1,9},{9... | collective-permute-start | bytes 817160 | tf_op jit(solution)/shard_map/ppermute | solution.py:211
  241.4 6.7 %collective-permute-start.27 = (bf16[112,1216]{1,0:T(8,128)(2,1)S(1)}, bf16[112,1216]{1,0:T(8,128)(2,1)S(1)}, u32[]{:S(2)}, u32[]{:S(2)}) collective-permute-start(bf16[112,1216]{1,0:T(8,128)(2,1)S(1)} %slice.41), channel_id=1, source_target_pairs={{8,0},{16,8},{24,16},{28,24},{20,28},{12,20},{4,12},{0,4},{9,1},{1... | collective-permute-start | bytes 817160 | tf_op jit(solution)/shard_map/ppermute | solution.py:215
  242.5 9.5 %collective-permute-start.30 = (bf16[192,1120]{1,0:T(8,128)(2,1)S(1)}, bf16[192,1120]{1,0:T(8,128)(2,1)S(1)}, u32[]{:S(2)}, u32[]{:S(2)}) collective-permute-start(bf16[192,1120]{1,0:T(8,128)(2,1)S(1)} %add_convert_fusion.2), channel_id=1, source_target_pairs={{0,2},{2,0},{1,3},{3,1},{4,6},{6,4},{5,7},{7,5},{8,10},{10,8},{9,1... | collective-permute-start | bytes 1290248 | tf_op jit(solution)/shard_map/ppermute | solution.py:362
  254.1 9.4 %collective-permute-start.33 = (bf16[192,672]{1,0:T(8,128)(2,1)}, bf16[192,672]{1,0:T(8,128)(2,1)}, u32[]{:S(2)}, u32[]{:S(2)}) collective-permute-start(bf16[192,672]{1,0:T(8,128)(2,1)} %add_convert_fusion.3), channel_id=1, source_target_pairs={{0,2},{2,0},{1,3},{3,1},{4,6},{6,4},{5,7},{7,5},{8,10},{10,8},{9,1... | collective-permute-start | bytes 774152 | tf_op jit(solution)/shard_map/ppermute | solution.py:362
  (38 other events, 472.7 us)

commit v2 on v0

--- a/solution.py
+++ b/solution.py
@@ -14,6 +14,7 @@
 HALO = 64
 LANES = 256
 VMEM_LIMIT = 48 * 1024 * 1024
+VMEM_MOST = 60 * 1024 * 1024
 NT = (((1,), (1,)), ((), ()))
 SMALL = pl.CostEstimate(flops=0, bytes_accessed=0, transcendentals=0)
 
@@ -282,7 +283,7 @@
             pltpu.VMEM((model, width), jnp.bfloat16),
             pltpu.SemaphoreType.DMA((2, len(pieces))),
         ],
-        compiler_params=pltpu.CompilerParams(vmem_limit_bytes=VMEM_LIMIT),
+        compiler_params=pltpu.CompilerParams(vmem_limit_bytes=VMEM_MOST),
         cost_estimate=SMALL,
     )(origins, *pieces, normed)
 

time: 263 us -> 260 us (0.989)
  local copies, waits for them, and re-layouts: 12.1 us -> 6.41 us
  waiting for transfers between devices: 95.5 us -> 98.4 us
    unnamed x65 -> x45, local copies, waits for them, and re-layouts: 9.43 us -> 3.18 us
  transfers between devices with their start and end apart: 35 -> 35, of which waited for: 17 -> 18; matrix products, arithmetic and copies ran while one was open for 8% -> 8% of each run, Pallas kernels for 21% -> 21%
where the time goes in v2:
time: 260 us; the launch traced here: 259 us
  waiting for transfers between devices  98.4 us (38%)
  Pallas kernels  58.1 us (22%)
  blocking collectives  40.9 us (16%)
  starting transfers between devices  36.2 us (14%)
  matrix products  15.7 us (6%)
  local copies, waits for them, and re-layouts  6.41 us (2%)
  other arithmetic  3.08 us (1%)
    ppermute x11, waiting for transfers between devices, step_forward(): self.forward.append(lax.ppermute(self.forward[-1][rows], 'req', self.pairs))  41.3 us
    psum x1, blocking collectives, per_device(): rank_feat = lax.psum(rank_part.astype(jnp.bfloat16), 'mdl')  40.9 us
    ppermute x11, waiting for transfers between devices, step_backward(): self.backward.append(lax.ppermute(self.backward[-1][rows], 'req', pairs))  36 us
    ppermute x4, waiting for transfers between devices, chip_swap(): return lax.ppermute(array, 'mdl', [(0, 2), (2, 0), (1, 3), (3, 1)])  20.4 us
    ppermute x11, starting transfers between devices, step_forward(): self.forward.append(lax.ppermute(self.forward[-1][rows], 'req', self.pairs))  19.9 us
    pallas_call x1, Pallas kernels, attention(): pl.pallas_call(attention_kernel, grid=(tokens // BLOCK,), in_specs=[own,...  15.6 us
    pallas_call x1, Pallas kernels, hidden_units(): pl.pallas_call(functools.partial(hidden_kernel, count), in_specs=[smem] +...  13 us
    pallas_call x1, Pallas kernels, project_and_normalise(): pl.pallas_call(project_kernel, in_specs=[smem] + [vmem] * 10, out_specs=[...  12.1 us
  transfers between devices with their start and end apart: 35, of which 18 were waited for; matrix products, arithmetic and copies ran while one was open for 8% of the time, Pallas kernels for 21%

profile of v2, /device:TPU:0, one launch (start us, length us, event | category | flops | bytes accessed | tf_op | source)
XLA Modules:
  0.0 259.3 jit_solution(4704385784645711913)
XLA Ops:
  0.0 1.6 slice_bitcast_fusion
  1.6 3.1 %collective-permute-start = (bf16[224,1216]{1,0:T(8,128)(2,1)S(1)}, bf16[224,1216]{1,0:T(8,128)(2,1)}, u32[]{:S(2)}, u32[]{:S(2)}) collective-permute-start(bf16[224,1216]{1,0:T(8,128)(2,1)S(1)} %get-tuple-element.100.refs_0_), channel_id=1, source_target_pairs={{0,8},{8,16},{16,24},{24,28},{28,20},{20,12},{12,4},{4,0},{1,9},{9... | collective-permute-start | bytes 1634312 | tf_op jit(solution)/shard_map/ppermute | solution.py:212
  4.7 2.0 collective-permute-start.2
  9.1 7.1 %shard_map.145 = bf16[8,2,2,448,128]{4,3,2,1,0:T(8,128)(2,1)S(1)} custom-call(s32[32]{0:T(128)S(1)} %reshape.124.table_ref, s32[32]{0:T(128)S(1)} %reshape.125.offset_ref, bf16[32,2,448,128]{3,2,1,0:T(8,128)(2,1)} %refs_3_.1, bf16[32,2,448,128]{3,2,1,0:T(8,128)(2,1)} %refs_3_.1, bf16[32,2,448,128]{3,2,1,0:T(8,128)(2,1)} %refs_3_.1, ...), custom_call_target="tpu_custom_call" | custom-call | tf_op jit(solution)/shard_map/pallas_call | solution.py:46
  16.2 1.8 copy-done.2
  18.6 2.2 collective-permute-done.1.refs_5_
  20.7 9.3 %collective-permute-done.2.refs_9_ = bf16[224,1216]{1,0:T(8,128)(2,1)} collective-permute-done((bf16[224,1216]{1,0:T(8,128)(2,1)S(1)}, bf16[224,1216]{1,0:T(8,128)(2,1)}, u32[]{:S(2)}, u32[]{:S(2)}) %collective-permute-start.2) | collective-permute-done | bytes 544800 | tf_op jit(solution)/shard_map/ppermute | solution.py:212
  31.5 4.8 %all-to-all-start = ((bf16[8,2,2,448,128]{4,3,2,1,0:T(8,128)(2,1)}), bf16[8,2,2,448,128]{4,3,2,1,0:T(8,128)(2,1)}, u32[]{:S(2)}, u32[]{:S(2)}) async-start(bf16[8,2,2,448,128]{4,3,2,1,0:T(8,128)(2,1)} %copy-done.2), calls=%async_computation | async-start | bytes 7340032 | tf_op jit(solution)/shard_map/all_to_all | solution.py:442
  38.1 2.7 %fusion.24 = f32[768,256]{0,1:S(1)} fusion(bf16[768,1792]{1,0:T(8,128)(2,1)} %refs_8_.1, bf16[1792,256]{0,1:T(8,128)(2,1)S(1)} %bitcast.62), kind=kOutput, calls=%fused_computation.55 | convolution fusion | flops 704643072 | bytes 4456448
  40.8 40.9 %psum.7 = bf16[768,16]{0,1:T(8,128)(2,1)S(1)} all-reduce(bf16[768,16]{0,1:T(8,128)(2,1)S(1)} %multiply_reduce_fusion), channel_id=1, replica_groups=mesh['req'=8,'mdl'=4] {'mdl'}, use_global_device_ids=true, to_apply=%region_7.8 | all-reduce | flops 12288 | bytes 49152 | tf_op jit(solution)/shard_map/psum | solution.py:459
  82.2 4.0 %fusion.4 = f32[768,448]{1,0:T(8,128)S(1)} fusion(bf16[768,1792]{1,0:T(8,128)(2,1)} %refs_8_.1, bf16[3,448,1792]{2,1,0:T(8,128)(2,1)} %param.16), kind=kOutput, calls=%fused_computation.4 | convolution fusion | flops 1233125376 | bytes 5734400 | tf_op jit(solution)/shard_map/dot_general | solution.py:445
  86.2 2.1 collective-permute-start.4
  90.1 3.0 %fusion = f32[768,448]{1,0:T(8,128)S(1)} fusion(bf16[768,1792]{1,0:T(8,128)(2,1)S(1)} %copy-done.4, bf16[3,448,1792]{2,1,0:T(8,128)(2,1)} %param.16), kind=kOutput, calls=%fused_computation | convolution fusion | flops 1233125376 | bytes 5734400 | tf_op jit(solution)/shard_map/dot_general | solution.py:445
  93.1 2.0 collective-permute-start.6
  95.2 14.6 %collective-permute-done.4.refs_2_ = bf16[224,1216]{1,0:T(8,128)(2,1)} collective-permute-done((bf16[224,1216]{1,0:T(8,128)(2,1)}, bf16[224,1216]{1,0:T(8,128)(2,1)}, u32[]{:S(2)}, u32[]{:S(2)}) %collective-permute-start.4) | collective-permute-done | bytes 544800 | tf_op jit(solution)/shard_map/ppermute | solution.py:212
  110.9 3.8 %fusion.9.key_before_ref.key_ref = bf16[768,448]{1,0:T(8,128)(2,1)S(1)} fusion(bf16[768,1792]{1,0:T(8,128)(2,1)} %refs_8_.1, bf16[3,448,1792]{2,1,0:T(8,128)(2,1)} %param.16), kind=kOutput, calls=%fused_computation.11 | convolution fusion | flops 1233469440 | bytes 5046272 | tf_op jit(solution)/shard_map/dot_general | solution.py:445
  114.8 11.9 %collective-permute-done.5.refs_6_ = bf16[224,1216]{1,0:T(8,128)(2,1)} collective-permute-done((bf16[224,1216]{1,0:T(8,128)(2,1)}, bf16[224,1216]{1,0:T(8,128)(2,1)}, u32[]{:S(2)}, u32[]{:S(2)}) %collective-permute-start.5) | collective-permute-done | bytes 544800 | tf_op jit(solution)/shard_map/ppermute | solution.py:216
  126.7 15.9 %collective-permute-done.7.refs_13_ = bf16[224,1216]{1,0:T(8,128)(2,1)} collective-permute-done((bf16[224,1216]{1,0:T(8,128)(2,1)}, bf16[224,1216]{1,0:T(8,128)(2,1)}, u32[]{:S(2)}, u32[]{:S(2)}) %collective-permute-start.7) | collective-permute-done | bytes 544800 | tf_op jit(solution)/shard_map/ppermute | solution.py:216
  142.5 2.5 collective-permute-start.11
  145.1 2.0 collective-permute-start.13
  147.8 15.6 %shard_map.146.refs_0_ = bf16[192,1792]{1,0:T(8,128)(2,1)S(1)} custom-call(bf16[768,448]{1,0:T(8,128)(2,1)S(1)} %add_convert_fusion.1.query_ref, bf16[768,448]{1,0:T(8,128)(2,1)S(1)} %fusion.9.key_before_ref.key_ref, bf16[768,448]{1,0:T(8,128)(2,1)S(1)} %fusion.9.key_before_ref.key_ref, bf16[768,448]{1,0:T(8,128)(2,1)S(1)} %add_convert_fusion.value_before_ref.value_ref, ...), custom_call_target="tpu_custom_call" | custom-call | tf_op jit(solution)/shard_map/pallas_call | solution.py:126
  163.4 6.0 %collective-permute-done.13.refs_11_ = bf16[224,1216]{1,0:T(8,128)(2,1)S(1)} collective-permute-done((bf16[224,1216]{1,0:T(8,128)(2,1)}, bf16[224,1216]{1,0:T(8,128)(2,1)S(1)}, u32[]{:S(2)}, u32[]{:S(2)}) %collective-permute-start.13) | collective-permute-done | bytes 544800 | tf_op jit(solution)/shard_map/ppermute | solution.py:212
  169.5 2.1 collective-permute-done.14.refs_14_
  175.1 12.0 %collective-permute-done.16.refs_2_ = bf16[192,1792]{1,0:T(8,128)(2,1)S(1)} collective-permute-done((bf16[192,1792]{1,0:T(8,128)(2,1)S(1)}, bf16[192,1792]{1,0:T(8,128)(2,1)S(1)}, u32[]{:S(2)}, u32[]{:S(2)}) %collective-permute-start.16) | collective-permute-done | bytes 688160 | tf_op jit(solution)/shard_map/ppermute | solution.py:363
  189.2 12.1 %shard_map.147 = (bf16[768,1792]{1,0:T(8,128)(2,1)}, bf16[192,1792]{1,0:T(8,128)(2,1)S(1)}) custom-call(s32[1]{0:T(128)} %bitcast.8.place_ref, bf16[192,1792]{1,0:T(8,128)(2,1)S(1)} %shard_map.146.refs_0_, bf16[192,1792]{1,0:T(8,128)(2,1)S(1)} %collective-permute-done.15.refs_1_, bf16[192,1792]{1,0:T(8,128)(2,1)S(1)} %collective-permute-done.16.refs_2_, ...), custom_call_target="tpu_custom_call" | custom-call | tf_op jit(solution)/shard_map/pallas_call | solution.py:179
  206.1 13.0 %shard_map.148.hidden_ref = bf16[768,1216]{1,0:T(8,128)(2,1)} custom-call(s32[16]{0:T(128)} %stack.58.origin_ref, bf16[224,1216]{1,0:T(8,128)(2,1)} %copy-done.5, bf16[224,1216]{1,0:T(8,128)(2,1)} %collective-permute-done.refs_1_, bf16[224,1216]{1,0:T(8,128)(2,1)} %collective-permute-done.4.refs_2_, bf16[224,1216]{1,0:T(8,128)(2,1)} %copy-done.7, ...), custom_call_target="tpu_custom_call" | custom-call | tf_op jit(solution)/shard_map/pallas_call | solution.py:276
  221.3 4.6 %shard_map.150 = (bf16[192,1120]{1,0:T(8,128)(2,1)S(1)}, bf16[192,1120]{1,0:T(8,128)(2,1)S(1)}, bf16[192,1120]{1,0:T(8,128)(2,1)S(1)}, bf16[192,1120]{1,0:T(8,128)(2,1)S(1)}) custom-call(bf16[768,1216]{1,0:T(8,128)(2,1)} %shard_map.148.hidden_ref, bf16[224,1216]{1,0:T(8,128)(2,1)S(1)} %get-tuple-element.73.refs_0_, ...), custom_call_target="tpu_custom_call" | custom-call | tf_op jit(solution)/shard_map/pallas_call | solution.py:312
  226.5 6.7 %collective-permute-done.24.refs_0_ = bf16[224,1216]{1,0:T(8,128)(2,1)S(1)} collective-permute-done((bf16[224,1216]{1,0:T(8,128)(2,1)}, bf16[224,1216]{1,0:T(8,128)(2,1)S(1)}, u32[]{:S(2)}, u32[]{:S(2)}) %collective-permute-start.24) | collective-permute-done | bytes 544800 | tf_op jit(solution)/shard_map/ppermute | solution.py:212
  237.0 2.9 %collective-permute-done.26.refs_2_ = bf16[112,1216]{1,0:T(8,128)(2,1)S(1)} collective-permute-done((bf16[112,1216]{1,0:T(8,128)(2,1)S(1)}, bf16[112,1216]{1,0:T(8,128)(2,1)S(1)}, u32[]{:S(2)}, u32[]{:S(2)}) %collective-permute-start.26) | collective-permute-done | bytes 272416 | tf_op jit(solution)/shard_map/ppermute | solution.py:212
  241.4 2.4 shard_map.149
  248.2 7.8 %collective-permute-done.33.refs_3_ = bf16[192,672]{1,0:T(8,128)(2,1)} collective-permute-done((bf16[192,672]{1,0:T(8,128)(2,1)}, bf16[192,672]{1,0:T(8,128)(2,1)}, u32[]{:S(2)}, u32[]{:S(2)}) %collective-permute-start.33) | collective-permute-done | bytes 258080 | tf_op jit(solution)/shard_map/ppermute | solution.py:363
  256.0 3.3 %shard_map.151 = bf16[192,1792]{1,0:T(8,128)(2,1)} custom-call(s32[8]{0:T(128)S(1)} %stack.56.origin_ref, bf16[192,1792]{1,0:T(8,128)(2,1)S(1)} %get-tuple-element.68.resid_ref, f32[192,1120]{1,0:T(8,128)S(1)} %convert_add_fusion.refs_0_, bf16[192,672]{1,0:T(8,128)(2,1)S(1)} %get-tuple-element.91.refs_1_, ...), custom_call_target="tpu_custom_call" | custom-call | tf_op jit(solution)/shard_map/pallas_call | solution.py:347
  (134 shorter events, 33.0 us)
Async XLA Ops:
  1.6 16.9 %collective-permute-start = (bf16[224,1216]{1,0:T(8,128)(2,1)S(1)}, bf16[224,1216]{1,0:T(8,128)(2,1)}, u32[]{:S(2)}, u32[]{:S(2)}) collective-permute-start(bf16[224,1216]{1,0:T(8,128)(2,1)S(1)} %get-tuple-element.100.refs_0_), channel_id=1, source_target_pairs={{0,8},{8,16},{16,24},{24,28},{28,20},{20,12},{12,4},{4,0},{1,9},{9... | collective-permute-start | bytes 1634312 | tf_op jit(solution)/shard_map/ppermute | solution.py:212
  4.7 16.0 %collective-permute-start.1 = (bf16[224,1216]{1,0:T(8,128)(2,1)S(1)}, bf16[224,1216]{1,0:T(8,128)(2,1)}, u32[]{:S(2)}, u32[]{:S(2)}) collective-permute-start(bf16[224,1216]{1,0:T(8,128)(2,1)S(1)} %get-tuple-element.100.refs_0_), channel_id=1, source_target_pairs={{8,0},{16,8},{24,16},{28,24},{20,28},{12,20},{4,12},{0,4},{9,1},{1... | collective-permute-start | bytes 1634312 | tf_op jit(solution)/shard_map/ppermute | solution.py:216
  4.7 25.3 %collective-permute-start.2 = (bf16[224,1216]{1,0:T(8,128)(2,1)S(1)}, bf16[224,1216]{1,0:T(8,128)(2,1)}, u32[]{:S(2)}, u32[]{:S(2)}) collective-permute-start(bf16[224,1216]{1,0:T(8,128)(2,1)S(1)} %get-tuple-element.101.refs_8_), channel_id=1, source_target_pairs={{0,8},{8,16},{16,24},{24,28},{28,20},{20,12},{12,4},{4,0},{1,9},{9... | collective-permute-start | bytes 1634312 | tf_op jit(solution)/shard_map/ppermute | solution.py:212
  6.7 24.8 %collective-permute-start.3 = (bf16[224,1216]{1,0:T(8,128)(2,1)S(1)}, bf16[224,1216]{1,0:T(8,128)(2,1)}, u32[]{:S(2)}, u32[]{:S(2)}) collective-permute-start(bf16[224,1216]{1,0:T(8,128)(2,1)S(1)} %get-tuple-element.101.refs_8_), channel_id=1, source_target_pairs={{8,0},{16,8},{24,16},{28,24},{20,28},{12,20},{4,12},{0,4},{9,1},{1... | collective-permute-start | bytes 1634312 | tf_op jit(solution)/shard_map/ppermute | solution.py:216
  31.5 111.0 %all-to-all-start = ((bf16[8,2,2,448,128]{4,3,2,1,0:T(8,128)(2,1)}), bf16[8,2,2,448,128]{4,3,2,1,0:T(8,128)(2,1)}, u32[]{:S(2)}, u32[]{:S(2)}) async-start(bf16[8,2,2,448,128]{4,3,2,1,0:T(8,128)(2,1)} %copy-done.2), calls=%async_computation | async-start | bytes 7340032 | tf_op jit(solution)/shard_map/all_to_all | solution.py:442
  36.4 106.2 %collective-permute-start.8 = (bf16[448,1792]{1,0:T(8,128)(2,1)}, bf16[448,1792]{1,0:T(8,128)(2,1)}, u32[]{:S(2)}, u32[]{:S(2)}) collective-permute-start(bf16[448,1792]{1,0:T(8,128)(2,1)} %refs_4_), channel_id=1, source_target_pairs={{0,1},{1,0},{2,3},{3,2},{4,5},{5,4},{6,7},{7,6},{8,9},{9,8},{10,11... | collective-permute-start | bytes 4816904 | tf_op jit(solution)/shard_map/ppermute | solution.py:359
  36.4 51.9 %collective-permute-start.9 = (bf16[448,1792]{1,0:T(8,128)(2,1)}, bf16[448,1792]{1,0:T(8,128)(2,1)}, u32[]{:S(2)}, u32[]{:S(2)}) collective-permute-start(bf16[448,1792]{1,0:T(8,128)(2,1)} %refs_4_), channel_id=1, source_target_pairs={{0,2},{2,0},{1,3},{3,1},{4,6},{6,4},{5,7},{7,5},{8,10},{10,8},{9,1... | collective-permute-start | bytes 4816904 | tf_op jit(solution)/shard_map/ppermute | solution.py:363
  86.2 23.6 %collective-permute-start.4 = (bf16[224,1216]{1,0:T(8,128)(2,1)}, bf16[224,1216]{1,0:T(8,128)(2,1)}, u32[]{:S(2)}, u32[]{:S(2)}) collective-permute-start(bf16[224,1216]{1,0:T(8,128)(2,1)} %collective-permute-done.refs_1_), channel_id=1, source_target_pairs={{0,8},{8,16},{16,24},{24,28},{28,20},{20,12},{12,4},{4,0},{1,9},{9... | collective-permute-start | bytes 1634312 | tf_op jit(solution)/shard_map/ppermute | solution.py:212
  88.3 54.3 %collective-permute-start.10 = (bf16[448,1792]{1,0:T(8,128)(2,1)}, bf16[448,1792]{1,0:T(8,128)(2,1)}, u32[]{:S(2)}, u32[]{:S(2)}) collective-permute-start(bf16[448,1792]{1,0:T(8,128)(2,1)} %collective-permute-done.9.refs_6_), channel_id=1, source_target_pairs={{0,1},{1,0},{2,3},{3,2},{4,5},{5,4},{6,7},{7,6},{8,9},{9,8},{10,11... | collective-permute-start | bytes 4816904 | tf_op jit(solution)/shard_map/ppermute | solution.py:359
  93.1 33.6 %collective-permute-start.5 = (bf16[224,1216]{1,0:T(8,128)(2,1)}, bf16[224,1216]{1,0:T(8,128)(2,1)}, u32[]{:S(2)}, u32[]{:S(2)}) collective-permute-start(bf16[224,1216]{1,0:T(8,128)(2,1)} %collective-permute-done.1.refs_5_), channel_id=1, source_target_pairs={{8,0},{16,8},{24,16},{28,24},{20,28},{12,20},{4,12},{0,4},{9,1},{1... | collective-permute-start | bytes 1634312 | tf_op jit(solution)/shard_map/ppermute | solution.py:216
  93.1 33.5 %collective-permute-start.6 = (bf16[224,1216]{1,0:T(8,128)(2,1)}, bf16[224,1216]{1,0:T(8,128)(2,1)}, u32[]{:S(2)}, u32[]{:S(2)}) collective-permute-start(bf16[224,1216]{1,0:T(8,128)(2,1)} %collective-permute-done.2.refs_9_), channel_id=1, source_target_pairs={{0,8},{8,16},{16,24},{24,28},{28,20},{20,12},{12,4},{4,0},{1,9},{9... | collective-permute-start | bytes 1634312 | tf_op jit(solution)/shard_map/ppermute | solution.py:212
  109.8 32.7 %collective-permute-start.7 = (bf16[224,1216]{1,0:T(8,128)(2,1)}, bf16[224,1216]{1,0:T(8,128)(2,1)}, u32[]{:S(2)}, u32[]{:S(2)}) collective-permute-start(bf16[224,1216]{1,0:T(8,128)(2,1)} %collective-permute-done.3.refs_12_), channel_id=1, source_target_pairs={{8,0},{16,8},{24,16},{28,24},{20,28},{12,20},{4,12},{0,4},{9,1},{1... | collective-permute-start | bytes 1634312 | tf_op jit(solution)/shard_map/ppermute | solution.py:216
  142.5 20.8 %collective-permute-start.11 = (bf16[224,1216]{1,0:T(8,128)(2,1)}, bf16[224,1216]{1,0:T(8,128)(2,1)S(1)}, u32[]{:S(2)}, u32[]{:S(2)}) collective-permute-start(bf16[224,1216]{1,0:T(8,128)(2,1)} %collective-permute-done.4.refs_2_), channel_id=1, source_target_pairs={{0,8},{8,16},{16,24},{24,28},{28,20},{20,12},{12,4},{4,0},{1,9},{9... | collective-permute-start | bytes 1634312 | tf_op jit(solution)/shard_map/ppermute | solution.py:212
  145.1 18.3 %collective-permute-start.12 = (bf16[224,1216]{1,0:T(8,128)(2,1)}, bf16[224,1216]{1,0:T(8,128)(2,1)S(1)}, u32[]{:S(2)}, u32[]{:S(2)}) collective-permute-start(bf16[224,1216]{1,0:T(8,128)(2,1)} %collective-permute-done.5.refs_6_), channel_id=1, source_target_pairs={{8,0},{16,8},{24,16},{28,24},{20,28},{12,20},{4,12},{0,4},{9,1},{1... | collective-permute-start | bytes 1634312 | tf_op jit(solution)/shard_map/ppermute | solution.py:216
  145.1 24.4 %collective-permute-start.13 = (bf16[224,1216]{1,0:T(8,128)(2,1)}, bf16[224,1216]{1,0:T(8,128)(2,1)S(1)}, u32[]{:S(2)}, u32[]{:S(2)}) collective-permute-start(bf16[224,1216]{1,0:T(8,128)(2,1)} %collective-permute-done.6.refs_10_), channel_id=1, source_target_pairs={{0,8},{8,16},{16,24},{24,28},{28,20},{20,12},{12,4},{4,0},{1,9},{9... | collective-permute-start | bytes 1634312 | tf_op jit(solution)/shard_map/ppermute | solution.py:212
  147.1 24.5 %collective-permute-start.14 = (bf16[224,1216]{1,0:T(8,128)(2,1)}, bf16[224,1216]{1,0:T(8,128)(2,1)S(1)}, u32[]{:S(2)}, u32[]{:S(2)}) collective-permute-start(bf16[224,1216]{1,0:T(8,128)(2,1)} %collective-permute-done.7.refs_13_), channel_id=1, source_target_pairs={{8,0},{16,8},{24,16},{28,24},{20,28},{12,20},{4,12},{0,4},{9,1},{1... | collective-permute-start | bytes 1634312 | tf_op jit(solution)/shard_map/ppermute | solution.py:216
  171.6 15.5 %collective-permute-start.16 = (bf16[192,1792]{1,0:T(8,128)(2,1)S(1)}, bf16[192,1792]{1,0:T(8,128)(2,1)S(1)}, u32[]{:S(2)}, u32[]{:S(2)}) collective-permute-start(bf16[192,1792]{1,0:T(8,128)(2,1)S(1)} %shard_map.146.refs_0_), channel_id=1, source_target_pairs={{0,2},{2,0},{1,3},{3,1},{4,6},{6,4},{5,7},{7,5},{8,10},{10,8},{9,1... | collective-permute-start | bytes 2064392 | tf_op jit(solution)/shard_map/ppermute | solution.py:363
  173.1 14.0 %collective-permute-start.18 = (bf16[224,1216]{1,0:T(8,128)(2,1)S(1)}, bf16[224,1216]{1,0:T(8,128)(2,1)S(1)}, u32[]{:S(2)}, u32[]{:S(2)}) collective-permute-start(bf16[224,1216]{1,0:T(8,128)(2,1)S(1)} %collective-permute-done.11.refs_3_), channel_id=1, source_target_pairs={{0,8},{8,16},{16,24},{24,28},{28,20},{20,12},{12,4},{4,0},{1,9},{9... | collective-permute-start | bytes 1634312 | tf_op jit(solution)/shard_map/ppermute | solution.py:212
  174.5 12.6 %collective-permute-start.19 = (bf16[224,1216]{1,0:T(8,128)(2,1)S(1)}, bf16[224,1216]{1,0:T(8,128)(2,1)S(1)}, u32[]{:S(2)}, u32[]{:S(2)}) collective-permute-start(bf16[224,1216]{1,0:T(8,128)(2,1)S(1)} %collective-permute-done.14.refs_14_), channel_id=1, source_target_pairs={{8,0},{16,8},{24,16},{28,24},{20,28},{12,20},{4,12},{0,4},{9,1},{1... | collective-permute-start | bytes 1634312 | tf_op jit(solution)/shard_map/ppermute | solution.py:216
  175.1 14.1 %collective-permute-start.15 = (bf16[192,1792]{1,0:T(8,128)(2,1)S(1)}, bf16[192,1792]{1,0:T(8,128)(2,1)S(1)}, u32[]{:S(2)}, u32[]{:S(2)}) collective-permute-start(bf16[192,1792]{1,0:T(8,128)(2,1)S(1)} %shard_map.146.refs_0_), channel_id=1, source_target_pairs={{0,1},{1,0},{2,3},{3,2},{4,5},{5,4},{6,7},{7,6},{8,9},{9,8},{10,11... | collective-permute-start | bytes 2064392 | tf_op jit(solution)/shard_map/ppermute | solution.py:359
  187.1 15.4 %collective-permute-start.20 = (bf16[224,1216]{1,0:T(8,128)(2,1)S(1)}, bf16[224,1216]{1,0:T(8,128)(2,1)S(1)}, u32[]{:S(2)}, u32[]{:S(2)}) collective-permute-start(bf16[224,1216]{1,0:T(8,128)(2,1)S(1)} %get-tuple-element.73.refs_0_), channel_id=1, source_target_pairs={{0,8},{8,16},{16,24},{24,28},{28,20},{20,12},{12,4},{4,0},{1,9},{9... | collective-permute-start | bytes 1634312 | tf_op jit(solution)/shard_map/ppermute | solution.py:212
  188.3 15.2 %collective-permute-start.21 = (bf16[224,1216]{1,0:T(8,128)(2,1)S(1)}, bf16[224,1216]{1,0:T(8,128)(2,1)}, u32[]{:S(2)}, u32[]{:S(2)}) collective-permute-start(bf16[224,1216]{1,0:T(8,128)(2,1)S(1)} %get-tuple-element.73.refs_0_), channel_id=1, source_target_pairs={{8,0},{16,8},{24,16},{28,24},{20,28},{12,20},{4,12},{0,4},{9,1},{1... | collective-permute-start | bytes 1634312 | tf_op jit(solution)/shard_map/ppermute | solution.py:216
  203.5 15.7 %collective-permute-start.22 = (bf16[224,1216]{1,0:T(8,128)(2,1)S(1)}, bf16[224,1216]{1,0:T(8,128)(2,1)}, u32[]{:S(2)}, u32[]{:S(2)}) collective-permute-start(bf16[224,1216]{1,0:T(8,128)(2,1)S(1)} %collective-permute-done.20.refs_1_), channel_id=1, source_target_pairs={{0,8},{8,16},{16,24},{24,28},{28,20},{20,12},{12,4},{4,0},{1,9},{9... | collective-permute-start | bytes 1634312 | tf_op jit(solution)/shard_map/ppermute | solution.py:212
  204.6 14.6 %collective-permute-start.23 = (bf16[224,1216]{1,0:T(8,128)(2,1)}, bf16[224,1216]{1,0:T(8,128)(2,1)S(1)}, u32[]{:S(2)}, u32[]{:S(2)}) collective-permute-start(bf16[224,1216]{1,0:T(8,128)(2,1)} %collective-permute-done.21.refs_3_), channel_id=1, source_target_pairs={{8,0},{16,8},{24,16},{28,24},{20,28},{12,20},{4,12},{0,4},{9,1},{1... | collective-permute-start | bytes 1634312 | tf_op jit(solution)/shard_map/ppermute | solution.py:216
  219.2 14.0 %collective-permute-start.24 = (bf16[224,1216]{1,0:T(8,128)(2,1)}, bf16[224,1216]{1,0:T(8,128)(2,1)S(1)}, u32[]{:S(2)}, u32[]{:S(2)}) collective-permute-start(bf16[224,1216]{1,0:T(8,128)(2,1)} %collective-permute-done.22.refs_2_), channel_id=1, source_target_pairs={{0,8},{8,16},{16,24},{24,28},{28,20},{20,12},{12,4},{4,0},{1,9},{9... | collective-permute-start | bytes 1634312 | tf_op jit(solution)/shard_map/ppermute | solution.py:212
  220.3 14.3 %collective-permute-start.25 = (bf16[224,1216]{1,0:T(8,128)(2,1)S(1)}, bf16[224,1216]{1,0:T(8,128)(2,1)S(1)}, u32[]{:S(2)}, u32[]{:S(2)}) collective-permute-start(bf16[224,1216]{1,0:T(8,128)(2,1)S(1)} %collective-permute-done.23.refs_4_), channel_id=1, source_target_pairs={{8,0},{16,8},{24,16},{28,24},{20,28},{12,20},{4,12},{0,4},{9,1},{1... | collective-permute-start | bytes 1634312 | tf_op jit(solution)/shard_map/ppermute | solution.py:216
  225.9 9.5 %collective-permute-start.29 = (bf16[192,1120]{1,0:T(8,128)(2,1)S(1)}, bf16[192,1120]{1,0:T(8,128)(2,1)S(1)}, u32[]{:S(2)}, u32[]{:S(2)}) collective-permute-start(bf16[192,1120]{1,0:T(8,128)(2,1)S(1)} %get-tuple-element.89), channel_id=1, source_target_pairs={{0,1},{1,0},{2,3},{3,2},{4,5},{5,4},{6,7},{7,6},{8,9},{9,8},{10,11... | collective-permute-start | bytes 1290248 | tf_op jit(solution)/shard_map/ppermute | solution.py:359
  226.0 18.4 %collective-permute-start.28 = (bf16[192,1120]{1,0:T(8,128)(2,1)S(1)}, bf16[192,1120]{1,0:T(8,128)(2,1)S(1)}, u32[]{:S(2)}, u32[]{:S(2)}) collective-permute-start(bf16[192,1120]{1,0:T(8,128)(2,1)S(1)} %get-tuple-element.87), channel_id=1, source_target_pairs={{0,1},{1,0},{2,3},{3,2},{4,5},{5,4},{6,7},{7,6},{8,9},{9,8},{10,11... | collective-permute-start | bytes 1290248 | tf_op jit(solution)/shard_map/ppermute | solution.py:359
  233.2 6.7 %collective-permute-start.26 = (bf16[112,1216]{1,0:T(8,128)(2,1)S(1)}, bf16[112,1216]{1,0:T(8,128)(2,1)S(1)}, u32[]{:S(2)}, u32[]{:S(2)}) collective-permute-start(bf16[112,1216]{1,0:T(8,128)(2,1)S(1)} %slice.40), channel_id=1, source_target_pairs={{0,8},{8,16},{16,24},{24,28},{28,20},{20,12},{12,4},{4,0},{1,9},{9... | collective-permute-start | bytes 817160 | tf_op jit(solution)/shard_map/ppermute | solution.py:212
  234.7 6.8 %collective-permute-start.27 = (bf16[112,1216]{1,0:T(8,128)(2,1)S(1)}, bf16[112,1216]{1,0:T(8,128)(2,1)S(1)}, u32[]{:S(2)}, u32[]{:S(2)}) collective-permute-start(bf16[112,1216]{1,0:T(8,128)(2,1)S(1)} %slice.41), channel_id=1, source_target_pairs={{8,0},{16,8},{24,16},{28,24},{20,28},{12,20},{4,12},{0,4},{9,1},{1... | collective-permute-start | bytes 817160 | tf_op jit(solution)/shard_map/ppermute | solution.py:216
  235.5 9.5 %collective-permute-start.30 = (bf16[192,1120]{1,0:T(8,128)(2,1)S(1)}, bf16[192,1120]{1,0:T(8,128)(2,1)S(1)}, u32[]{:S(2)}, u32[]{:S(2)}) collective-permute-start(bf16[192,1120]{1,0:T(8,128)(2,1)S(1)} %add_convert_fusion.2), channel_id=1, source_target_pairs={{0,2},{2,0},{1,3},{3,1},{4,6},{6,4},{5,7},{7,5},{8,10},{10,8},{9,1... | collective-permute-start | bytes 1290248 | tf_op jit(solution)/shard_map/ppermute | solution.py:363
  246.6 9.4 %collective-permute-start.33 = (bf16[192,672]{1,0:T(8,128)(2,1)}, bf16[192,672]{1,0:T(8,128)(2,1)}, u32[]{:S(2)}, u32[]{:S(2)}) collective-permute-start(bf16[192,672]{1,0:T(8,128)(2,1)} %add_convert_fusion.3), channel_id=1, source_target_pairs={{0,2},{2,0},{1,3},{3,1},{4,6},{6,4},{5,7},{7,5},{8,10},{10,8},{9,1... | collective-permute-start | bytes 774152 | tf_op jit(solution)/shard_map/ppermute | solution.py:363
  (25 other events, 431.3 us)

commit v3 on v2

--- a/solution.py
+++ b/solution.py
@@ -529,9 +529,9 @@
         near_terms = own, other
         far_cost = pl.CostEstimate(flops=1 << 33, bytes_accessed=0, transcendentals=0)
         own, other, keep, send = down_sums(far_pieces, hidden, far_cost)
-        keep, near_sum = lax.optimization_barrier((keep, sum_here(*near_terms, across)))
+        keep, across = lax.optimization_barrier((keep, across))
         part = sum_on_chip(keep, send)
-        groups = [near_sum], [own, core_swap(other), chip_swap(part)]
+        groups = [near_terms[0], core_swap(near_terms[1]), across], [own, core_swap(other), chip_swap(part)]
         return place_and_add(down_origins, resid, groups, rows_held)
 
     mixed = attention(query_rows, key_rows, value_rows, start_of, slot_of, prefix)

time: 260 us -> 261 us (level)
  local copies, waits for them, and re-layouts: 6.41 us -> 10.6 us
    unnamed x45 -> x57, local copies, waits for them, and re-layouts: 3.18 us -> 7.31 us
  transfers between devices with their start and end apart: 35 -> 35, of which waited for: 18 -> 17; matrix products, arithmetic and copies ran while one was open for 8% -> 8% of each run, Pallas kernels for 21% -> 21%
where the time goes in v3:
time: 261 us; the launch traced here: 260 us
  waiting for transfers between devices  96.3 us (37%)
  Pallas kernels  57.9 us (22%)
  blocking collectives  40.9 us (16%)
  starting transfers between devices  35.7 us (14%)
  matrix products  15.7 us (6%)
  local copies, waits for them, and re-layouts  10.6 us (4%)
  other arithmetic  2.83 us (1%)
    psum x1, blocking collectives, per_device(): rank_feat = lax.psum(rank_part.astype(jnp.bfloat16), 'mdl')  40.9 us
    ppermute x11, waiting for transfers between devices, step_forward(): self.forward.append(lax.ppermute(self.forward[-1][rows], 'req', self.pairs))  40.5 us
    ppermute x11, waiting for transfers between devices, step_backward(): self.backward.append(lax.ppermute(self.backward[-1][rows], 'req', pairs))  35.8 us
    ppermute x4, waiting for transfers between devices, chip_swap(): return lax.ppermute(array, 'mdl', [(0, 2), (2, 0), (1, 3), (3, 1)])  19.9 us
    ppermute x11, starting transfers between devices, step_forward(): self.forward.append(lax.ppermute(self.forward[-1][rows], 'req', self.pairs))  19.8 us
    pallas_call x1, Pallas kernels, attention(): pl.pallas_call(attention_kernel, grid=(tokens // BLOCK,), in_specs=[own,...  15.6 us
    pallas_call x1, Pallas kernels, hidden_units(): pl.pallas_call(functools.partial(hidden_kernel, count), in_specs=[smem] +...  13 us
    pallas_call x1, Pallas kernels, project_and_normalise(): pl.pallas_call(project_kernel, in_specs=[smem] + [vmem] * 10, out_specs=[...  12.1 us
  transfers between devices with their start and end apart: 35, of which 17 were waited for; matrix products, arithmetic and copies ran while one was open for 8% of the time, Pallas kernels for 21%

profile of v3, /device:TPU:0, one launch (start us, length us, event | category | flops | bytes accessed | tf_op | source)
XLA Modules:
  0.0 260.4 jit_solution(12890942056617508784)
XLA Ops:
  0.0 1.6 slice_bitcast_fusion
  1.6 3.1 %collective-permute-start = (bf16[224,1216]{1,0:T(8,128)(2,1)S(1)}, bf16[224,1216]{1,0:T(8,128)(2,1)}, u32[]{:S(2)}, u32[]{:S(2)}) collective-permute-start(bf16[224,1216]{1,0:T(8,128)(2,1)S(1)} %get-tuple-element.100.refs_0_), channel_id=1, source_target_pairs={{0,8},{8,16},{16,24},{24,28},{28,20},{20,12},{12,4},{4,0},{1,9},{9... | collective-permute-start | bytes 1634312 | tf_op jit(solution)/shard_map/ppermute | solution.py:212
  4.7 2.0 collective-permute-start.2
  9.0 7.3 %shard_map.145 = bf16[8,2,2,448,128]{4,3,2,1,0:T(8,128)(2,1)S(1)} custom-call(s32[32]{0:T(128)S(1)} %reshape.124.table_ref, s32[32]{0:T(128)S(1)} %reshape.125.offset_ref, bf16[32,2,448,128]{3,2,1,0:T(8,128)(2,1)} %refs_3_.1, bf16[32,2,448,128]{3,2,1,0:T(8,128)(2,1)} %refs_3_.1, bf16[32,2,448,128]{3,2,1,0:T(8,128)(2,1)} %refs_3_.1, ...), custom_call_target="tpu_custom_call" | custom-call | tf_op jit(solution)/shard_map/pallas_call | solution.py:46
  16.4 1.8 copy-done.2
  18.6 2.2 collective-permute-done.1.refs_5_
  20.7 9.3 %collective-permute-done.2.refs_9_ = bf16[224,1216]{1,0:T(8,128)(2,1)} collective-permute-done((bf16[224,1216]{1,0:T(8,128)(2,1)S(1)}, bf16[224,1216]{1,0:T(8,128)(2,1)}, u32[]{:S(2)}, u32[]{:S(2)}) %collective-permute-start.2) | collective-permute-done | bytes 544800 | tf_op jit(solution)/shard_map/ppermute | solution.py:212
  31.5 4.8 %all-to-all-start = ((bf16[8,2,2,448,128]{4,3,2,1,0:T(8,128)(2,1)}), bf16[8,2,2,448,128]{4,3,2,1,0:T(8,128)(2,1)}, u32[]{:S(2)}, u32[]{:S(2)}) async-start(bf16[8,2,2,448,128]{4,3,2,1,0:T(8,128)(2,1)} %copy-done.2), calls=%async_computation | async-start | bytes 7340032 | tf_op jit(solution)/shard_map/all_to_all | solution.py:442
  38.1 2.7 %fusion.24 = f32[768,256]{0,1:S(1)} fusion(bf16[768,1792]{1,0:T(8,128)(2,1)} %refs_8_.1, bf16[1792,256]{0,1:T(8,128)(2,1)S(1)} %bitcast.62), kind=kOutput, calls=%fused_computation.54 | convolution fusion | flops 704643072 | bytes 4456448
  40.8 40.9 %psum.7 = bf16[768,16]{0,1:T(8,128)(2,1)S(1)} all-reduce(bf16[768,16]{0,1:T(8,128)(2,1)S(1)} %multiply_reduce_fusion), channel_id=1, replica_groups=mesh['req'=8,'mdl'=4] {'mdl'}, use_global_device_ids=true, to_apply=%region_7.8 | all-reduce | flops 12288 | bytes 49152 | tf_op jit(solution)/shard_map/psum | solution.py:459
  82.2 4.0 %fusion.4 = f32[768,448]{1,0:T(8,128)S(1)} fusion(bf16[768,1792]{1,0:T(8,128)(2,1)} %refs_8_.1, bf16[3,448,1792]{2,1,0:T(8,128)(2,1)} %param.16), kind=kOutput, calls=%fused_computation.4 | convolution fusion | flops 1233125376 | bytes 5734400 | tf_op jit(solution)/shard_map/dot_general | solution.py:445
  86.2 2.1 collective-permute-start.4
  90.1 3.0 %fusion = f32[768,448]{1,0:T(8,128)S(1)} fusion(bf16[768,1792]{1,0:T(8,128)(2,1)S(1)} %copy-done.10, bf16[3,448,1792]{2,1,0:T(8,128)(2,1)} %param.16), kind=kOutput, calls=%fused_computation | convolution fusion | flops 1233125376 | bytes 5734400 | tf_op jit(solution)/shard_map/dot_general | solution.py:445
  93.1 2.0 collective-permute-start.6
  95.2 14.6 %collective-permute-done.4.refs_2_ = bf16[224,1216]{1,0:T(8,128)(2,1)} collective-permute-done((bf16[224,1216]{1,0:T(8,128)(2,1)}, bf16[224,1216]{1,0:T(8,128)(2,1)}, u32[]{:S(2)}, u32[]{:S(2)}) %collective-permute-start.4) | collective-permute-done | bytes 544800 | tf_op jit(solution)/shard_map/ppermute | solution.py:212
  110.9 3.8 %fusion.9.key_before_ref.key_ref = bf16[768,448]{1,0:T(8,128)(2,1)S(1)} fusion(bf16[768,1792]{1,0:T(8,128)(2,1)} %refs_8_.1, bf16[3,448,1792]{2,1,0:T(8,128)(2,1)} %param.16), kind=kOutput, calls=%fused_computation.11 | convolution fusion | flops 1233469440 | bytes 5046272 | tf_op jit(solution)/shard_map/dot_general | solution.py:445
  114.8 11.9 %collective-permute-done.5.refs_6_ = bf16[224,1216]{1,0:T(8,128)(2,1)} collective-permute-done((bf16[224,1216]{1,0:T(8,128)(2,1)}, bf16[224,1216]{1,0:T(8,128)(2,1)}, u32[]{:S(2)}, u32[]{:S(2)}) %collective-permute-start.5) | collective-permute-done | bytes 544800 | tf_op jit(solution)/shard_map/ppermute | solution.py:216
  126.7 15.9 %collective-permute-done.7.refs_13_ = bf16[224,1216]{1,0:T(8,128)(2,1)} collective-permute-done((bf16[224,1216]{1,0:T(8,128)(2,1)}, bf16[224,1216]{1,0:T(8,128)(2,1)}, u32[]{:S(2)}, u32[]{:S(2)}) %collective-permute-start.7) | collective-permute-done | bytes 544800 | tf_op jit(solution)/shard_map/ppermute | solution.py:216
  142.5 2.5 collective-permute-start.11
  145.1 2.0 collective-permute-start.13
  147.8 15.6 %shard_map.146.refs_0_ = bf16[192,1792]{1,0:T(8,128)(2,1)S(1)} custom-call(bf16[768,448]{1,0:T(8,128)(2,1)S(1)} %add_convert_fusion.1.query_ref, bf16[768,448]{1,0:T(8,128)(2,1)S(1)} %fusion.9.key_before_ref.key_ref, bf16[768,448]{1,0:T(8,128)(2,1)S(1)} %fusion.9.key_before_ref.key_ref, bf16[768,448]{1,0:T(8,128)(2,1)S(1)} %add_convert_fusion.value_before_ref.value_ref, ...), custom_call_target="tpu_custom_call" | custom-call | tf_op jit(solution)/shard_map/pallas_call | solution.py:126
  163.4 6.0 %collective-permute-done.13.refs_11_ = bf16[224,1216]{1,0:T(8,128)(2,1)S(1)} collective-permute-done((bf16[224,1216]{1,0:T(8,128)(2,1)}, bf16[224,1216]{1,0:T(8,128)(2,1)S(1)}, u32[]{:S(2)}, u32[]{:S(2)}) %collective-permute-start.13) | collective-permute-done | bytes 544800 | tf_op jit(solution)/shard_map/ppermute | solution.py:212
  169.5 2.1 collective-permute-done.14.refs_14_
  175.1 12.0 %collective-permute-done.16.refs_2_ = bf16[192,1792]{1,0:T(8,128)(2,1)S(1)} collective-permute-done((bf16[192,1792]{1,0:T(8,128)(2,1)S(1)}, bf16[192,1792]{1,0:T(8,128)(2,1)S(1)}, u32[]{:S(2)}, u32[]{:S(2)}) %collective-permute-start.16) | collective-permute-done | bytes 688160 | tf_op jit(solution)/shard_map/ppermute | solution.py:363
  189.2 12.1 %shard_map.147 = (bf16[768,1792]{1,0:T(8,128)(2,1)}, bf16[192,1792]{1,0:T(8,128)(2,1)S(1)}) custom-call(s32[1]{0:T(128)} %bitcast.8.place_ref, bf16[192,1792]{1,0:T(8,128)(2,1)S(1)} %shard_map.146.refs_0_, bf16[192,1792]{1,0:T(8,128)(2,1)S(1)} %collective-permute-done.15.refs_1_, bf16[192,1792]{1,0:T(8,128)(2,1)S(1)} %collective-permute-done.16.refs_2_, ...), custom_call_target="tpu_custom_call" | custom-call | tf_op jit(solution)/shard_map/pallas_call | solution.py:179
  206.1 13.0 %shard_map.148.hidden_ref = bf16[768,1216]{1,0:T(8,128)(2,1)} custom-call(s32[16]{0:T(128)} %stack.58.origin_ref, bf16[224,1216]{1,0:T(8,128)(2,1)} %copy-done.11, bf16[224,1216]{1,0:T(8,128)(2,1)} %collective-permute-done.refs_1_, bf16[224,1216]{1,0:T(8,128)(2,1)} %collective-permute-done.4.refs_2_, bf16[224,1216]{1,0:T(8,128)(2,1)} %copy-done.13, ...), custom_call_target="tpu_custom_call" | custom-call | tf_op jit(solution)/shard_map/pallas_call | solution.py:276
  221.2 5.1 %shard_map.149 = (bf16[192,1120]{1,0:T(8,128)(2,1)S(1)}, bf16[192,1120]{1,0:T(8,128)(2,1)}, bf16[192,1120]{1,0:T(8,128)(2,1)S(1)}, bf16[192,1120]{1,0:T(8,128)(2,1)S(1)}) custom-call(bf16[768,1216]{1,0:T(8,128)(2,1)} %shard_map.148.hidden_ref, bf16[224,1216]{1,0:T(8,128)(2,1)S(1)} %get-tuple-element.73.refs_0_, ...), custom_call_target="tpu_custom_call" | custom-call | tf_op jit(solution)/shard_map/pallas_call | solution.py:312
  227.1 6.0 %collective-permute-done.25.refs_0_ = bf16[224,1216]{1,0:T(8,128)(2,1)S(1)} collective-permute-done((bf16[224,1216]{1,0:T(8,128)(2,1)}, bf16[224,1216]{1,0:T(8,128)(2,1)S(1)}, u32[]{:S(2)}, u32[]{:S(2)}) %collective-permute-start.25) | collective-permute-done | bytes 544800 | tf_op jit(solution)/shard_map/ppermute | solution.py:212
  237.0 2.9 %collective-permute-done.27.refs_2_ = bf16[112,1216]{1,0:T(8,128)(2,1)S(1)} collective-permute-done((bf16[112,1216]{1,0:T(8,128)(2,1)S(1)}, bf16[112,1216]{1,0:T(8,128)(2,1)S(1)}, u32[]{:S(2)}, u32[]{:S(2)}) %collective-permute-start.27) | collective-permute-done | bytes 272416 | tf_op jit(solution)/shard_map/ppermute | solution.py:212
  241.3 1.8 shard_map.150
  248.0 6.8 %collective-permute-done.33.refs_5_ = bf16[192,672]{1,0:T(8,128)(2,1)S(1)} collective-permute-done((bf16[192,672]{1,0:T(8,128)(2,1)}, bf16[192,672]{1,0:T(8,128)(2,1)S(1)}, u32[]{:S(2)}, u32[]{:S(2)}) %collective-permute-start.33) | collective-permute-done | bytes 258080 | tf_op jit(solution)/shard_map/ppermute | solution.py:363
  257.5 2.9 %shard_map.151 = bf16[192,1792]{1,0:T(8,128)(2,1)} custom-call(s32[8]{0:T(128)S(1)} %stack.56.origin_ref, bf16[192,1792]{1,0:T(8,128)(2,1)S(1)} %get-tuple-element.68.resid_ref, bf16[192,1120]{1,0:T(8,128)(2,1)S(1)} %copy-done.5, bf16[192,1120]{1,0:T(8,128)(2,1)S(1)} %collective-permute-done.24.refs_1_, ...), custom_call_target="tpu_custom_call" | custom-call | tf_op jit(solution)/shard_map/pallas_call | solution.py:347
  (145 shorter events, 36.0 us)
Async XLA Ops:
  1.6 16.9 %collective-permute-start = (bf16[224,1216]{1,0:T(8,128)(2,1)S(1)}, bf16[224,1216]{1,0:T(8,128)(2,1)}, u32[]{:S(2)}, u32[]{:S(2)}) collective-permute-start(bf16[224,1216]{1,0:T(8,128)(2,1)S(1)} %get-tuple-element.100.refs_0_), channel_id=1, source_target_pairs={{0,8},{8,16},{16,24},{24,28},{28,20},{20,12},{12,4},{4,0},{1,9},{9... | collective-permute-start | bytes 1634312 | tf_op jit(solution)/shard_map/ppermute | solution.py:212
  4.7 16.0 %collective-permute-start.1 = (bf16[224,1216]{1,0:T(8,128)(2,1)S(1)}, bf16[224,1216]{1,0:T(8,128)(2,1)}, u32[]{:S(2)}, u32[]{:S(2)}) collective-permute-start(bf16[224,1216]{1,0:T(8,128)(2,1)S(1)} %get-tuple-element.100.refs_0_), channel_id=1, source_target_pairs={{8,0},{16,8},{24,16},{28,24},{20,28},{12,20},{4,12},{0,4},{9,1},{1... | collective-permute-start | bytes 1634312 | tf_op jit(solution)/shard_map/ppermute | solution.py:216
  4.7 25.3 %collective-permute-start.2 = (bf16[224,1216]{1,0:T(8,128)(2,1)S(1)}, bf16[224,1216]{1,0:T(8,128)(2,1)}, u32[]{:S(2)}, u32[]{:S(2)}) collective-permute-start(bf16[224,1216]{1,0:T(8,128)(2,1)S(1)} %get-tuple-element.101.refs_8_), channel_id=1, source_target_pairs={{0,8},{8,16},{16,24},{24,28},{28,20},{20,12},{12,4},{4,0},{1,9},{9... | collective-permute-start | bytes 1634312 | tf_op jit(solution)/shard_map/ppermute | solution.py:212
  6.7 24.8 %collective-permute-start.3 = (bf16[224,1216]{1,0:T(8,128)(2,1)S(1)}, bf16[224,1216]{1,0:T(8,128)(2,1)}, u32[]{:S(2)}, u32[]{:S(2)}) collective-permute-start(bf16[224,1216]{1,0:T(8,128)(2,1)S(1)} %get-tuple-element.101.refs_8_), channel_id=1, source_target_pairs={{8,0},{16,8},{24,16},{28,24},{20,28},{12,20},{4,12},{0,4},{9,1},{1... | collective-permute-start | bytes 1634312 | tf_op jit(solution)/shard_map/ppermute | solution.py:216
  31.5 111.0 %all-to-all-start = ((bf16[8,2,2,448,128]{4,3,2,1,0:T(8,128)(2,1)}), bf16[8,2,2,448,128]{4,3,2,1,0:T(8,128)(2,1)}, u32[]{:S(2)}, u32[]{:S(2)}) async-start(bf16[8,2,2,448,128]{4,3,2,1,0:T(8,128)(2,1)} %copy-done.2), calls=%async_computation | async-start | bytes 7340032 | tf_op jit(solution)/shard_map/all_to_all | solution.py:442
  36.4 106.2 %collective-permute-start.8 = (bf16[448,1792]{1,0:T(8,128)(2,1)}, bf16[448,1792]{1,0:T(8,128)(2,1)}, u32[]{:S(2)}, u32[]{:S(2)}) collective-permute-start(bf16[448,1792]{1,0:T(8,128)(2,1)} %refs_4_), channel_id=1, source_target_pairs={{0,1},{1,0},{2,3},{3,2},{4,5},{5,4},{6,7},{7,6},{8,9},{9,8},{10,11... | collective-permute-start | bytes 4816904 | tf_op jit(solution)/shard_map/ppermute | solution.py:359
  36.4 51.9 %collective-permute-start.9 = (bf16[448,1792]{1,0:T(8,128)(2,1)}, bf16[448,1792]{1,0:T(8,128)(2,1)}, u32[]{:S(2)}, u32[]{:S(2)}) collective-permute-start(bf16[448,1792]{1,0:T(8,128)(2,1)} %refs_4_), channel_id=1, source_target_pairs={{0,2},{2,0},{1,3},{3,1},{4,6},{6,4},{5,7},{7,5},{8,10},{10,8},{9,1... | collective-permute-start | bytes 4816904 | tf_op jit(solution)/shard_map/ppermute | solution.py:363
  86.2 23.6 %collective-permute-start.4 = (bf16[224,1216]{1,0:T(8,128)(2,1)}, bf16[224,1216]{1,0:T(8,128)(2,1)}, u32[]{:S(2)}, u32[]{:S(2)}) collective-permute-start(bf16[224,1216]{1,0:T(8,128)(2,1)} %collective-permute-done.refs_1_), channel_id=1, source_target_pairs={{0,8},{8,16},{16,24},{24,28},{28,20},{20,12},{12,4},{4,0},{1,9},{9... | collective-permute-start | bytes 1634312 | tf_op jit(solution)/shard_map/ppermute | solution.py:212
  88.3 54.3 %collective-permute-start.10 = (bf16[448,1792]{1,0:T(8,128)(2,1)}, bf16[448,1792]{1,0:T(8,128)(2,1)}, u32[]{:S(2)}, u32[]{:S(2)}) collective-permute-start(bf16[448,1792]{1,0:T(8,128)(2,1)} %collective-permute-done.9.refs_6_), channel_id=1, source_target_pairs={{0,1},{1,0},{2,3},{3,2},{4,5},{5,4},{6,7},{7,6},{8,9},{9,8},{10,11... | collective-permute-start | bytes 4816904 | tf_op jit(solution)/shard_map/ppermute | solution.py:359
  93.1 33.6 %collective-permute-start.5 = (bf16[224,1216]{1,0:T(8,128)(2,1)}, bf16[224,1216]{1,0:T(8,128)(2,1)}, u32[]{:S(2)}, u32[]{:S(2)}) collective-permute-start(bf16[224,1216]{1,0:T(8,128)(2,1)} %collective-permute-done.1.refs_5_), channel_id=1, source_target_pairs={{8,0},{16,8},{24,16},{28,24},{20,28},{12,20},{4,12},{0,4},{9,1},{1... | collective-permute-start | bytes 1634312 | tf_op jit(solution)/shard_map/ppermute | solution.py:216
  93.1 33.5 %collective-permute-start.6 = (bf16[224,1216]{1,0:T(8,128)(2,1)}, bf16[224,1216]{1,0:T(8,128)(2,1)}, u32[]{:S(2)}, u32[]{:S(2)}) collective-permute-start(bf16[224,1216]{1,0:T(8,128)(2,1)} %collective-permute-done.2.refs_9_), channel_id=1, source_target_pairs={{0,8},{8,16},{16,24},{24,28},{28,20},{20,12},{12,4},{4,0},{1,9},{9... | collective-permute-start | bytes 1634312 | tf_op jit(solution)/shard_map/ppermute | solution.py:212
  109.8 32.7 %collective-permute-start.7 = (bf16[224,1216]{1,0:T(8,128)(2,1)}, bf16[224,1216]{1,0:T(8,128)(2,1)}, u32[]{:S(2)}, u32[]{:S(2)}) collective-permute-start(bf16[224,1216]{1,0:T(8,128)(2,1)} %collective-permute-done.3.refs_12_), channel_id=1, source_target_pairs={{8,0},{16,8},{24,16},{28,24},{20,28},{12,20},{4,12},{0,4},{9,1},{1... | collective-permute-start | bytes 1634312 | tf_op jit(solution)/shard_map/ppermute | solution.py:216
  142.5 20.8 %collective-permute-start.11 = (bf16[224,1216]{1,0:T(8,128)(2,1)}, bf16[224,1216]{1,0:T(8,128)(2,1)S(1)}, u32[]{:S(2)}, u32[]{:S(2)}) collective-permute-start(bf16[224,1216]{1,0:T(8,128)(2,1)} %collective-permute-done.4.refs_2_), channel_id=1, source_target_pairs={{0,8},{8,16},{16,24},{24,28},{28,20},{20,12},{12,4},{4,0},{1,9},{9... | collective-permute-start | bytes 1634312 | tf_op jit(solution)/shard_map/ppermute | solution.py:212
  145.1 18.3 %collective-permute-start.12 = (bf16[224,1216]{1,0:T(8,128)(2,1)}, bf16[224,1216]{1,0:T(8,128)(2,1)S(1)}, u32[]{:S(2)}, u32[]{:S(2)}) collective-permute-start(bf16[224,1216]{1,0:T(8,128)(2,1)} %collective-permute-done.5.refs_6_), channel_id=1, source_target_pairs={{8,0},{16,8},{24,16},{28,24},{20,28},{12,20},{4,12},{0,4},{9,1},{1... | collective-permute-start | bytes 1634312 | tf_op jit(solution)/shard_map/ppermute | solution.py:216
  145.1 24.4 %collective-permute-start.13 = (bf16[224,1216]{1,0:T(8,128)(2,1)}, bf16[224,1216]{1,0:T(8,128)(2,1)S(1)}, u32[]{:S(2)}, u32[]{:S(2)}) collective-permute-start(bf16[224,1216]{1,0:T(8,128)(2,1)} %collective-permute-done.6.refs_10_), channel_id=1, source_target_pairs={{0,8},{8,16},{16,24},{24,28},{28,20},{20,12},{12,4},{4,0},{1,9},{9... | collective-permute-start | bytes 1634312 | tf_op jit(solution)/shard_map/ppermute | solution.py:212
  147.1 24.5 %collective-permute-start.14 = (bf16[224,1216]{1,0:T(8,128)(2,1)}, bf16[224,1216]{1,0:T(8,128)(2,1)S(1)}, u32[]{:S(2)}, u32[]{:S(2)}) collective-permute-start(bf16[224,1216]{1,0:T(8,128)(2,1)} %collective-permute-done.7.refs_13_), channel_id=1, source_target_pairs={{8,0},{16,8},{24,16},{28,24},{20,28},{12,20},{4,12},{0,4},{9,1},{1... | collective-permute-start | bytes 1634312 | tf_op jit(solution)/shard_map/ppermute | solution.py:216
  171.6 15.5 %collective-permute-start.16 = (bf16[192,1792]{1,0:T(8,128)(2,1)S(1)}, bf16[192,1792]{1,0:T(8,128)(2,1)S(1)}, u32[]{:S(2)}, u32[]{:S(2)}) collective-permute-start(bf16[192,1792]{1,0:T(8,128)(2,1)S(1)} %shard_map.146.refs_0_), channel_id=1, source_target_pairs={{0,2},{2,0},{1,3},{3,1},{4,6},{6,4},{5,7},{7,5},{8,10},{10,8},{9,1... | collective-permute-start | bytes 2064392 | tf_op jit(solution)/shard_map/ppermute | solution.py:363
  173.1 14.0 %collective-permute-start.18 = (bf16[224,1216]{1,0:T(8,128)(2,1)S(1)}, bf16[224,1216]{1,0:T(8,128)(2,1)S(1)}, u32[]{:S(2)}, u32[]{:S(2)}) collective-permute-start(bf16[224,1216]{1,0:T(8,128)(2,1)S(1)} %collective-permute-done.11.refs_3_), channel_id=1, source_target_pairs={{0,8},{8,16},{16,24},{24,28},{28,20},{20,12},{12,4},{4,0},{1,9},{9... | collective-permute-start | bytes 1634312 | tf_op jit(solution)/shard_map/ppermute | solution.py:212
  174.5 12.6 %collective-permute-start.19 = (bf16[224,1216]{1,0:T(8,128)(2,1)S(1)}, bf16[224,1216]{1,0:T(8,128)(2,1)S(1)}, u32[]{:S(2)}, u32[]{:S(2)}) collective-permute-start(bf16[224,1216]{1,0:T(8,128)(2,1)S(1)} %collective-permute-done.14.refs_14_), channel_id=1, source_target_pairs={{8,0},{16,8},{24,16},{28,24},{20,28},{12,20},{4,12},{0,4},{9,1},{1... | collective-permute-start | bytes 1634312 | tf_op jit(solution)/shard_map/ppermute | solution.py:216
  175.1 14.1 %collective-permute-start.15 = (bf16[192,1792]{1,0:T(8,128)(2,1)S(1)}, bf16[192,1792]{1,0:T(8,128)(2,1)S(1)}, u32[]{:S(2)}, u32[]{:S(2)}) collective-permute-start(bf16[192,1792]{1,0:T(8,128)(2,1)S(1)} %shard_map.146.refs_0_), channel_id=1, source_target_pairs={{0,1},{1,0},{2,3},{3,2},{4,5},{5,4},{6,7},{7,6},{8,9},{9,8},{10,11... | collective-permute-start | bytes 2064392 | tf_op jit(solution)/shard_map/ppermute | solution.py:359
  187.1 15.4 %collective-permute-start.20 = (bf16[224,1216]{1,0:T(8,128)(2,1)S(1)}, bf16[224,1216]{1,0:T(8,128)(2,1)S(1)}, u32[]{:S(2)}, u32[]{:S(2)}) collective-permute-start(bf16[224,1216]{1,0:T(8,128)(2,1)S(1)} %get-tuple-element.73.refs_0_), channel_id=1, source_target_pairs={{0,8},{8,16},{16,24},{24,28},{28,20},{20,12},{12,4},{4,0},{1,9},{9... | collective-permute-start | bytes 1634312 | tf_op jit(solution)/shard_map/ppermute | solution.py:212
  188.3 15.1 %collective-permute-start.21 = (bf16[224,1216]{1,0:T(8,128)(2,1)S(1)}, bf16[224,1216]{1,0:T(8,128)(2,1)S(1)}, u32[]{:S(2)}, u32[]{:S(2)}) collective-permute-start(bf16[224,1216]{1,0:T(8,128)(2,1)S(1)} %get-tuple-element.73.refs_0_), channel_id=1, source_target_pairs={{8,0},{16,8},{24,16},{28,24},{20,28},{12,20},{4,12},{0,4},{9,1},{1... | collective-permute-start | bytes 1634312 | tf_op jit(solution)/shard_map/ppermute | solution.py:216
  203.4 15.7 %collective-permute-start.22 = (bf16[224,1216]{1,0:T(8,128)(2,1)S(1)}, bf16[224,1216]{1,0:T(8,128)(2,1)}, u32[]{:S(2)}, u32[]{:S(2)}) collective-permute-start(bf16[224,1216]{1,0:T(8,128)(2,1)S(1)} %collective-permute-done.20.refs_1_), channel_id=1, source_target_pairs={{0,8},{8,16},{16,24},{24,28},{28,20},{20,12},{12,4},{4,0},{1,9},{9... | collective-permute-start | bytes 1634312 | tf_op jit(solution)/shard_map/ppermute | solution.py:212
  204.4 14.7 %collective-permute-start.23 = (bf16[224,1216]{1,0:T(8,128)(2,1)S(1)}, bf16[224,1216]{1,0:T(8,128)(2,1)S(1)}, u32[]{:S(2)}, u32[]{:S(2)}) collective-permute-start(bf16[224,1216]{1,0:T(8,128)(2,1)S(1)} %collective-permute-done.21.refs_3_), channel_id=1, source_target_pairs={{8,0},{16,8},{24,16},{28,24},{20,28},{12,20},{4,12},{0,4},{9,1},{1... | collective-permute-start | bytes 1634312 | tf_op jit(solution)/shard_map/ppermute | solution.py:216
  219.1 14.0 %collective-permute-start.25 = (bf16[224,1216]{1,0:T(8,128)(2,1)}, bf16[224,1216]{1,0:T(8,128)(2,1)S(1)}, u32[]{:S(2)}, u32[]{:S(2)}) collective-permute-start(bf16[224,1216]{1,0:T(8,128)(2,1)} %collective-permute-done.22.refs_2_), channel_id=1, source_target_pairs={{0,8},{8,16},{16,24},{24,28},{28,20},{20,12},{12,4},{4,0},{1,9},{9... | collective-permute-start | bytes 1634312 | tf_op jit(solution)/shard_map/ppermute | solution.py:212
  220.2 14.3 %collective-permute-start.26 = (bf16[224,1216]{1,0:T(8,128)(2,1)S(1)}, bf16[224,1216]{1,0:T(8,128)(2,1)S(1)}, u32[]{:S(2)}, u32[]{:S(2)}) collective-permute-start(bf16[224,1216]{1,0:T(8,128)(2,1)S(1)} %collective-permute-done.23.refs_4_), channel_id=1, source_target_pairs={{8,0},{16,8},{24,16},{28,24},{20,28},{12,20},{4,12},{0,4},{9,1},{1... | collective-permute-start | bytes 1634312 | tf_op jit(solution)/shard_map/ppermute | solution.py:216
  227.1 8.2 %collective-permute-start.29 = (bf16[192,1120]{1,0:T(8,128)(2,1)S(1)}, bf16[192,1120]{1,0:T(8,128)(2,1)S(1)}, u32[]{:S(2)}, u32[]{:S(2)}) collective-permute-start(bf16[192,1120]{1,0:T(8,128)(2,1)S(1)} %get-tuple-element.89), channel_id=1, source_target_pairs={{0,1},{1,0},{2,3},{3,2},{4,5},{5,4},{6,7},{7,6},{8,9},{9,8},{10,11... | collective-permute-start | bytes 1290248 | tf_op jit(solution)/shard_map/ppermute | solution.py:359
  233.1 6.7 %collective-permute-start.27 = (bf16[112,1216]{1,0:T(8,128)(2,1)S(1)}, bf16[112,1216]{1,0:T(8,128)(2,1)S(1)}, u32[]{:S(2)}, u32[]{:S(2)}) collective-permute-start(bf16[112,1216]{1,0:T(8,128)(2,1)S(1)} %slice.40), channel_id=1, source_target_pairs={{0,8},{8,16},{16,24},{24,28},{28,20},{20,12},{12,4},{4,0},{1,9},{9... | collective-permute-start | bytes 817160 | tf_op jit(solution)/shard_map/ppermute | solution.py:212
  234.5 6.7 %collective-permute-start.28 = (bf16[112,1216]{1,0:T(8,128)(2,1)S(1)}, bf16[112,1216]{1,0:T(8,128)(2,1)S(1)}, u32[]{:S(2)}, u32[]{:S(2)}) collective-permute-start(bf16[112,1216]{1,0:T(8,128)(2,1)S(1)} %slice.41), channel_id=1, source_target_pairs={{8,0},{16,8},{24,16},{28,24},{20,28},{12,20},{4,12},{0,4},{9,1},{1... | collective-permute-start | bytes 817160 | tf_op jit(solution)/shard_map/ppermute | solution.py:216
  235.4 9.5 %collective-permute-start.30 = (bf16[192,1120]{1,0:T(8,128)(2,1)S(1)}, bf16[192,1120]{1,0:T(8,128)(2,1)S(1)}, u32[]{:S(2)}, u32[]{:S(2)}) collective-permute-start(bf16[192,1120]{1,0:T(8,128)(2,1)S(1)} %add_convert_fusion.2), channel_id=1, source_target_pairs={{0,2},{2,0},{1,3},{3,1},{4,6},{6,4},{5,7},{7,5},{8,10},{10,8},{9,1... | collective-permute-start | bytes 1290248 | tf_op jit(solution)/shard_map/ppermute | solution.py:363
  243.2 4.1 %collective-permute-start.24 = (bf16[192,1120]{1,0:T(8,128)(2,1)}, bf16[192,1120]{1,0:T(8,128)(2,1)S(1)}, u32[]{:S(2)}, u32[]{:S(2)}) collective-permute-start(bf16[192,1120]{1,0:T(8,128)(2,1)} %get-tuple-element.86), channel_id=1, source_target_pairs={{0,1},{1,0},{2,3},{3,2},{4,5},{5,4},{6,7},{7,6},{8,9},{9,8},{10,11... | collective-permute-start | bytes 1290248 | tf_op jit(solution)/shard_map/ppermute | solution.py:359
  245.7 9.1 %collective-permute-start.33 = (bf16[192,672]{1,0:T(8,128)(2,1)}, bf16[192,672]{1,0:T(8,128)(2,1)S(1)}, u32[]{:S(2)}, u32[]{:S(2)}) collective-permute-start(bf16[192,672]{1,0:T(8,128)(2,1)} %add_convert_fusion.3), channel_id=1, source_target_pairs={{0,2},{2,0},{1,3},{3,1},{4,6},{6,4},{5,7},{7,5},{8,10},{10,8},{9,1... | collective-permute-start | bytes 774152 | tf_op jit(solution)/shard_map/ppermute | solution.py:363
  (31 other events, 444.8 us)
